TPU v7x, 128 devices: a whole 4x4x4 slice. The times are simulated.
128 devices in a mesh: ulysses: 4 (over z), blk: 8 (over y, core), tensor: 4 (over x).
Axes of the slice: x: 4, y: 4, z: 4, core: 2. Of those that a mesh axis runs over, the one named last changes fastest.
Arguments:
- tokens: bfloat16 [8192, 5120], P(('ulysses', 'blk'), 'tensor'), may hold values from -20 to 20
- w_qkv: bfloat16 [5120, 3, 4096], P(None, None, ('ulysses', 'tensor')), may hold values from -2 to 2
- qkv_scale: float32 [3, 32], P(None, ('ulysses', 'tensor')), may hold values from 0.6 to 9
- block_mask: int32 [32, 64, 64], P(('ulysses', 'tensor')), may hold values from 0 to 1, as said below
- w_out: bfloat16 [4, 1024, 5120], P(None, 'tensor'), may hold values from -0.125 to 0.125
Outputs:
- mixed: bfloat16 [8192, 5120], P(('ulysses', 'blk'), 'tensor')
Inputs may be any that keep to these rules, and one draw needn't show every extreme that they name: `block_mask`: 0 or 1; the share of ones differs from head to head.
All inputs are finite; a program needn't handle non-finite values.
Results may differ from a plain program's by a relative error of at most 0.015.
Values may be sent and summed in bfloat16 or wider, within the bound.
No kernel may reach another device: no remote copies, remote signals or barrier semaphores. Data moves between devices by JAX's collectives and lax.ppermute only.
A program may use at most 128 MiB of HBM per device.

v0:
```python
import functools
import math

import jax
import jax.numpy as jnp
from jax import lax
from jax.experimental import pallas as pl
from jax.experimental.pallas import tpu as pltpu
from jax.sharding import PartitionSpec as P

HD = 128
BLOCK = 128
NEG = -1e30
LOG2E = 1.4426950408889634
OFFSETS = (0, -1, 1, 2)
CONTRACT_LAST = (((1,), (1,)), ((), ()))


def ring(n, step):
    return [(i, (i + step) % n) for i in range(n)]


def y_ring(n, step):
    return [(i, (i + 2 * step) % n) for i in range(n)]


def core_swap(n):
    return [(i, i ^ 1) for i in range(n)]


def emit_heads(acc, scale_ref, core, q_ref, kv_ref, give_ref):
    scaled = (acc * scale_ref[...]).astype(jnp.bfloat16)
    heads = [[scaled[:, c * 256 + h * HD : c * 256 + (h + 1) * HD] for c in range(3)] for h in (0, 1)]
    is_first = core == 0

    @pl.when(is_first)
    def _():
        q_ref[...] = heads[0][0]
        kv_ref[...] = jnp.concatenate(heads[0][1:], axis=1)
        give_ref[...] = jnp.concatenate(heads[1], axis=1)

    @pl.when(jnp.logical_not(is_first))
    def _():
        q_ref[...] = heads[1][0]
        kv_ref[...] = jnp.concatenate(heads[1][1:], axis=1)
        give_ref[...] = jnp.concatenate(heads[0], axis=1)


def heads_shape(rows):
    return [jax.ShapeDtypeStruct((rows, n * HD), jnp.bfloat16) for n in (1, 2, 3)]


def load_kernel(pick, where_ref, hbm, o_ref, sems):
    copies = []
    for i in range(o_ref.shape[0]):
        copies.append(pltpu.make_async_copy(pick(hbm, where_ref[i]), o_ref.at[i], sems.at[i]))
        copies[-1].start()
    for copy in copies:
        copy.wait()


def load(where, w, shape, pick, limit):
    return pl.pallas_call(
        functools.partial(load_kernel, pick),
        in_specs=[pl.BlockSpec(memory_space=pltpu.SMEM), pl.BlockSpec(memory_space=pltpu.HBM)],
        out_specs=VM,
        out_shape=jax.ShapeDtypeStruct((4,) + shape, w.dtype),
        scratch_shapes=[pltpu.SemaphoreType.DMA((4,))],
        compiler_params=pltpu.CompilerParams(vmem_limit_bytes=limit << 20),
        cost_estimate=pl.CostEstimate(flops=0, bytes_accessed=w.size * 4, transcendentals=0),
    )(where, w)


def stage_kernel(n_a, b_slices, n_done, has_part, emit_all, where_ref, w_ref, scale_ref, *refs):
    a_refs, refs = refs[:n_a], refs[n_a:]
    b_refs, refs = refs[: len(b_slices)], refs[len(b_slices) :]
    done_refs, refs = refs[:n_done], refs[n_done:]
    part_refs, refs = refs[:has_part], refs[has_part:]
    outs, acc_ref = refs[:-1], refs[-1]
    feat = w_ref.shape[2]
    na = sum(r.shape[0] for r in a_refs)
    fresh = not has_part
    for i in range(4):
        x = [r[:, i * feat : (i + 1) * feat] for r in a_refs]
        x += [r[...] for r, s in zip(b_refs, b_slices) if s == i]
        with_b = len(x) > n_a
        x = jnp.concatenate(x, axis=0) if len(x) > 1 else x[0]
        for c in range(3):
            cols = slice(c * 256, (c + 1) * 256)
            d = jnp.dot(x, w_ref[i, c], preferred_element_type=jnp.float32)
            acc_ref[:na, cols] = d[:na] if i == 0 else acc_ref[:na, cols] + d[:na]
            if with_b:
                first = i == min(b_slices)
                before = None if first and fresh else part_refs[0][:, cols] if first else acc_ref[na:, cols]
                acc_ref[na:, cols] = d[na:] if before is None else before + d[na:]
    if not emit_all and not n_done:
        outs[0][...] = acc_ref[:na]
        outs[1][...] = acc_ref[na:]
        return
    rows = acc_ref[...] if emit_all else acc_ref[:na]
    if n_done:
        rows = jnp.concatenate([done_refs[0][...], rows], axis=0)
    emit_heads(rows, scale_ref, where_ref[4], *outs[:3])
    if not emit_all:
        outs[3][...] = acc_ref[na:]


VM = pl.BlockSpec(memory_space=pltpu.VMEM)
FIXED = [pl.BlockSpec(memory_space=pltpu.SMEM), VM, VM]


def project_stage(where, w, scale, a_parts, b_parts, b_slices, done, part, emit_all):
    feat = w.shape[2]
    na = sum(x.shape[0] for x in a_parts)
    nb = 512 if part is None else part.shape[0]
    f32 = lambda n: jax.ShapeDtypeStruct((n, 768), jnp.float32)
    if emit_all:
        shapes = heads_shape(na + nb)
    elif done is not None:
        shapes = heads_shape(done.shape[0] + na) + [f32(nb)]
    else:
        shapes = [f32(na), f32(nb)]
    extra = [x for x in (done, part) if x is not None]
    return pl.pallas_call(
        functools.partial(
            stage_kernel, len(a_parts), b_slices, int(done is not None), int(part is not None), emit_all
        ),
        in_specs=FIXED + [VM] * (len(a_parts) + len(b_parts) + len(extra)),
        out_specs=[VM] * len(shapes),
        out_shape=shapes,
        scratch_shapes=[pltpu.VMEM((na + nb, 768), jnp.float32)],
        compiler_params=pltpu.CompilerParams(vmem_limit_bytes=16 << 20),
        cost_estimate=pl.CostEstimate(
            flops=2 * 768 * feat * (4 * na + sum(x.shape[0] for x in b_parts)),
            bytes_accessed=w.size * 2,
            transcendentals=0,
        ),
    )(where, w, scale, *a_parts, *b_parts, *extra)


def out_kernel(places, where_ref, *refs):
    xs, w_ref, outs = refs[:4], refs[4], refs[5:]
    per_place = len(outs) // len(places)
    for n, place in enumerate(places):
        d = sum(
            jnp.dot(x_ref[...], w_ref[place, where_ref[5 + i]], preferred_element_type=jnp.float32)
            for i, x_ref in enumerate(xs)
        )
        at = 0
        for o_ref in outs[n * per_place : (n + 1) * per_place]:
            o_ref[...] = d[at : at + o_ref.shape[0]].astype(o_ref.dtype)
            at += o_ref.shape[0]


def out_project(where, xs, w, places, dtype, pieces):
    rows, cols = xs[0].shape[0], w.shape[3]
    n = len(places) * pieces
    return pl.pallas_call(
        functools.partial(out_kernel, places),
        in_specs=[pl.BlockSpec(memory_space=pltpu.SMEM)] + [VM] * 5,
        out_specs=[VM] * n,
        out_shape=[jax.ShapeDtypeStruct((rows // pieces, cols), dtype)] * n,
        compiler_params=pltpu.CompilerParams(vmem_limit_bytes=16 << 20),
        cost_estimate=pl.CostEstimate(
            flops=2 * len(places) * rows * 1024 * cols, bytes_accessed=n * 4 * rows * cols, transcendentals=0
        ),
    )(where, *xs, w)


def attn_kernel(sizes, first_block, begin, end, q_ref, qm_ref, *refs):
    if not begin:
        state_refs, refs = refs[:3], refs[3:]
    kv_refs, outs = refs[: len(sizes)], refs[len(sizes) :]
    rows = q_ref.shape[0]
    q = jnp.concatenate([q_ref[...], qm_ref[...]], axis=1)
    tiles = []
    for kv_ref, bk in zip(kv_refs, sizes):
        for j in range(0, kv_ref.shape[0], bk):
            tiles.append((kv_ref, slice(j, j + bk), bk, first_block))
            first_block += bk // BLOCK

    def score(tile):
        kv_ref, at, bk, block = tile
        lane = lax.broadcasted_iota(jnp.int32, (bk, HD), 1)
        inner = lax.broadcasted_iota(jnp.int32, (bk, HD), 0) // BLOCK
        onehot = (lane == inner + block).astype(jnp.float32).astype(jnp.bfloat16)
        k = jnp.concatenate([kv_ref[at, :HD], onehot], axis=1)
        return lax.dot_general(q, k, CONTRACT_LAST, preferred_element_type=jnp.float32)

    s = score(tiles[0])
    for i, (kv_ref, at, bk, _) in enumerate(tiles):
        s_next = score(tiles[i + 1]) if i + 1 < len(tiles) else None
        top = jnp.max(s, axis=1, keepdims=True)
        v = jnp.concatenate([kv_ref[at, HD:], jnp.ones((bk, HD), jnp.bfloat16)], axis=1)
        fresh = begin and i == 0
        if fresh:
            high = jnp.broadcast_to(top, (rows, HD))
        else:
            if i == 0:
                old = state_refs[2][...]
                acc = jnp.concatenate([state_refs[0][...], state_refs[1][...]], axis=1)
            else:
                old = high
            high = jnp.maximum(old, top)
        p = jnp.exp2(s - jnp.concatenate([high] * (bk // HD), axis=1)).astype(jnp.bfloat16)
        d = jnp.dot(p, v, preferred_element_type=jnp.float32)
        if fresh:
            acc = d
        else:
            factor = jnp.exp2(old - high)
            acc = acc * jnp.concatenate([factor, factor], axis=1) + d
        s = s_next
    if end:
        outs[0][...] = (acc[:, :HD] / acc[:, HD:]).astype(jnp.bfloat16)
    else:
        outs[0][...] = acc[:, :HD]
        outs[1][...] = acc[:, HD:]
        outs[2][...] = high


def attention(q, qm, kvs, sizes, first_block, state, end, bq=1024):
    rows = q.shape[0]
    keys = sum(kv.shape[0] for kv in kvs)
    begin = state is None
    block = pl.BlockSpec((bq, HD), lambda i: (i, 0))
    f32 = jax.ShapeDtypeStruct((rows, HD), jnp.float32)
    return pl.pallas_call(
        functools.partial(attn_kernel, sizes, first_block, begin, end),
        grid=(rows // bq,),
        in_specs=[block] * (2 if begin else 5)
        + [pl.BlockSpec(kv.shape, lambda i: (0, 0)) for kv in kvs],
        out_specs=block if end else [block] * 3,
        out_shape=jax.ShapeDtypeStruct((rows, HD), jnp.bfloat16) if end else [f32] * 3,
        compiler_params=pltpu.CompilerParams(vmem_limit_bytes=28 << 20),
        cost_estimate=pl.CostEstimate(
            flops=8 * rows * keys * HD, bytes_accessed=keys * 512, transcendentals=rows * keys
        ),
    )(q, qm, *([] if begin else state), *kvs)


def local(tokens, w_qkv, qkv_scale, block_mask, w_out):
    nu, nb, nt = lax.axis_size("ulysses"), lax.axis_size("blk"), lax.axis_size("tensor")
    u, b, t = lax.axis_index("ulysses"), lax.axis_index("blk"), lax.axis_index("tensor")
    y, core = b // 2, b % 2
    half = tokens.shape[0] // 2
    quarter = half // 2
    pp = lax.ppermute
    offsets = jnp.array(OFFSETS, jnp.int32)

    def direct(value, axis, n):
        return [value] + [pp(value, axis, ring(n, s)) for s in (1, -1, 2)]

    where = jnp.concatenate([(t + offsets) % nt, core[None], (u - offsets) % nu])
    feat = tokens.shape[1]

    def at_rows(ref, i):
        return ref.at[:, pl.ds(pl.multiple_of(i * feat, feat), feat), :]

    def at_cols(ref, i):
        return ref.at[:, :, pl.ds(pl.multiple_of(i * feat, feat), feat)]

    hold = lax.optimization_barrier
    w = load(where, jnp.transpose(w_qkv, (1, 0, 2)), (3, feat, w_qkv.shape[2]), at_rows, 46)
    w_o = load(where, w_out, w_out.shape[:2] + (feat,), at_cols, 34)
    scale = qkv_scale * jnp.array([LOG2E / math.sqrt(HD), 1.0, 1.0], jnp.float32)[:, None]
    scale = jnp.repeat(scale.reshape(1, 6), HD, axis=1)

    ny = nb // 2
    groups = (u + offsets) % nu
    cores = jnp.stack([core, 1 - core])

    def block_id(yy, slot, group, odd):
        return (groups[group] * nb + 2 * (yy % ny) + cores[slot]) * 2 + odd

    early = [(g, 0) for g in range(3)]
    late = [(3, 0)] + [(g, 1) for g in range(4)]
    def ring_order(part):
        own = [(y, s) + g for s in (0, 1) for g in part]
        near = [(y + o, s) + g for o in (-1, 1) for s in (0, 1) for g in part]
        far = [(y + 2, s) + g for s in (0, 1) for g in part]
        return own, near, far

    early_ids, late_ids = ring_order(early), ring_order(late)
    keys = sum(early_ids, []) + sum(late_ids, [])
    key_ids = jnp.stack([block_id(*k) for k in keys])
    query_ids = jnp.stack(
        [block_id(y, s, g, odd) for s in (0, 1) for odd in (0, 1) for g in range(4)]
    )
    blocks = jnp.arange(block_mask.shape[1], dtype=jnp.int32)
    key_hot = (key_ids[:, None] == blocks[None, :]).astype(jnp.float32)
    query_hot = (query_ids[:, None] == blocks[None, :]).astype(jnp.float32)
    mask = lax.dynamic_index_in_dim(block_mask, core, 0, keepdims=False).astype(jnp.float32)
    live = query_hot @ mask @ key_hot.T > 0.5
    live = live | (query_ids[:, None] == key_ids[None, :])
    bias = jnp.where(live, 0.0, NEG).astype(jnp.bfloat16)
    bias = jnp.pad(bias, ((0, 0), (0, HD - bias.shape[1])))
    bias = jnp.repeat(bias, BLOCK, axis=0)

    a_own = jnp.concatenate(direct(tokens[:half], "tensor", nt), axis=1)
    b_parts, w = hold((direct(tokens[half:], "ulysses", nu), w))
    b_own = jnp.concatenate(b_parts, axis=0)
    a_m = pp(a_own, "ulysses", ring(nu, 1))
    b_m = pp(b_own, "tensor", ring(nt, 1))
    a_p = pp(a_own, "ulysses", ring(nu, -1))
    b_p = pp(b_own, "tensor", ring(nt, -1))
    ah, bh = a_own.shape[0] // 2, b_own.shape[0] // 2
    a0 = pp(a_m[:ah], "ulysses", ring(nu, 1))
    a1 = pp(a_p[ah:], "ulysses", ring(nu, -1))
    b0 = pp(b_m[:bh], "tensor", ring(nt, 1))
    b1 = pp(b_p[bh:], "tensor", ring(nt, -1))

    def swap(kv, give):
        got = pp(give, "blk", core_swap(nb))
        return got[:, :HD], jnp.concatenate([kv, got[:, HD:]], axis=0)

    def near_y(kv):
        return [pp(kv, "blk", y_ring(nb, s)) for s in (1, -1)]

    def far_y(kv_m, kv_p):
        h = kv_m.shape[0] // 2
        return [pp(kv_m[:h], "blk", y_ring(nb, 1)), pp(kv_p[h:], "blk", y_ring(nb, -1))]

    done, part = project_stage(where, w, scale, [a_own], [b_own], (0,), None, None, False)
    done, bias, w_o = hold((done, bias, w_o))
    q1, kv1, give1, part = project_stage(
        where, w, scale, [a_m, a_p], [b_m, b_p], (1, 2), done, part, False
    )
    q1x, kv1 = swap(kv1, give1)
    kv1_near = near_y(kv1)
    q2, kv2, give2 = project_stage(where, w, scale, [a0, a1], [b0, b1], (3, 3), None, part, True)
    give2, kv1_near = hold((give2, kv1_near))
    q2x, kv2 = swap(kv2, give2)
    kv1_far = far_y(*kv1_near)
    kv2_near = near_y(kv2)
    kv2_far = far_y(*kv2_near)

    q = jnp.concatenate([q1, q2, q1x, q2x], axis=0)
    state = attention(q, bias, [kv1] + kv1_near, (768,) * 3, 0, None, False)
    state = attention(q, bias, kv1_far + [kv2], (384, 384, 640), 18, state, False)
    state = attention(q, bias, kv2_near, (640, 640), 34, state, False)
    out = attention(q, bias, kv2_far, (640, 640), 54, state, True)

    out = out.reshape(2, 2, nu, half, HD)
    other = pp(out[1], "blk", core_swap(nb))
    mine = out[0]
    first = jnp.where(core == 0, mine, other)
    second = jnp.where(core == 0, other, mine)
    heads = jnp.concatenate([first, second], axis=-1)
    heads = [heads[:, g].reshape(2 * half, 2 * HD) for g in range(nu)]
    arrived = [heads[0]] + [
        pp(heads[i], "ulysses", ring(nu, OFFSETS[i])) for i in range(1, nu)
    ]
    bf = jnp.bfloat16
    far_0, far_1 = out_project(where, arrived, w_o, (3,), bf, 2)
    rows = 2 * half
    hr = rows // 2
    far_m = pp(far_0, "tensor", ring(nt, 1))
    far_p = pp(far_1, "tensor", ring(nt, -1))
    to_m, to_p = out_project(where, arrived, w_o, (1, 2), jnp.float32, 1)
    to_p = jnp.concatenate([to_p[:hr] + far_m.astype(jnp.float32), to_p[hr:]], axis=0).astype(bf)
    to_m = jnp.concatenate([to_m[:hr], to_m[hr:] + far_p.astype(jnp.float32)], axis=0).astype(bf)
    from_m = pp(to_p, "tensor", ring(nt, 1))
    from_p = pp(to_m, "tensor", ring(nt, -1))
    (own,) = out_project(where, arrived, w_o, (0,), jnp.float32, 1)
    return (own + from_m.astype(jnp.float32) + from_p.astype(jnp.float32)).astype(bf)


def solution(mesh):
    return jax.shard_map(
        local,
        mesh=mesh,
        in_specs=(
            P(("ulysses", "blk"), "tensor"),
            P(None, None, ("ulysses", "tensor")),
            P(None, ("ulysses", "tensor")),
            P(("ulysses", "tensor"), None, None),
            P(None, "tensor", None),
        ),
        out_specs=P(("ulysses", "blk"), "tensor"),
        check_vma=False,
    )
```

profile of v0, /device:TPU:0, one launch (start us, length us, event | category | flops | bytes accessed | tf_op | source)
XLA Modules:
  0.0 170.6 jit_solution(4570316481596554136)
XLA Ops:
  10.6 3.9 %shard_map.73.w_ref = bf16[4,3,1280,256]{3,2,1,0:T(8,128)(2,1)S(1)} custom-call(s32[9]{0:T(128)S(1)} %pad_add_fusion.where_ref, bf16[3,5120,256]{2,1,0:T(8,128)(2,1)} %bitcast.97), custom_call_target="tpu_custom_call" | custom-call | bytes 15728640 | tf_op jit(solution)/shard_map/pallas_call | solution.py:63
  14.5 3.1 %copy-done.2 = bf16[4,3,1280,256]{3,2,1,0:T(8,128)(2,1)} copy-done((bf16[4,3,1280,256]{3,2,1,0:T(8,128)(2,1)}, bf16[4,3,1280,256]{3,2,1,0:T(8,128)(2,1)S(1)}, u32[]{:S(2)}) %copy-start.2) | copy-done | bytes 7864344
  36.1 4.7 %shard_map.75.refs_4_ = bf16[4,4,256,1280]{3,2,1,0:T(8,128)(2,1)S(1)} custom-call(s32[9]{0:T(128)S(1)} %pad_add_fusion.where_ref, bf16[4,256,5120]{2,1,0:T(8,128)(2,1)} %hbm.1), custom_call_target="tpu_custom_call" | custom-call | bytes 20971520 | tf_op jit(solution)/shard_map/pallas_call | solution.py:63
  40.8 4.0 %copy-done = bf16[4,4,256,1280]{3,2,1,0:T(8,128)(2,1)} copy-done((bf16[4,4,256,1280]{3,2,1,0:T(8,128)(2,1)}, bf16[4,4,256,1280]{3,2,1,0:T(8,128)(2,1)S(1)}, u32[]{:S(2)}) %copy-start) | copy-done | bytes 10485784
  45.4 3.2 %copy-done.3 = bf16[4,3,1280,256]{3,2,1,0:T(8,128)(2,1)S(1)} copy-done((bf16[4,3,1280,256]{3,2,1,0:T(8,128)(2,1)S(1)}, bf16[4,3,1280,256]{3,2,1,0:T(8,128)(2,1)}, u32[]{:S(2)}) %copy-start.3) | copy-done | bytes 7864344
  48.6 3.6 %shard_map.74 = (f32[128,768]{1,0:T(8,128)S(1)}, f32[512,768]{1,0:T(8,128)S(1)}) custom-call(s32[9]{0:T(128)S(1)} %pad_add_fusion.where_ref, bf16[4,3,1280,256]{3,2,1,0:T(8,128)(2,1)S(1)} %copy-done.3, f32[1,768]{1,0:T(1,128)S(1)} %bitcast.94, bf16[128,5120]{1,0:T(8,128)(2,1)S(1)} %pad_maximum_fusion.refs_0_, ...), custom_call_target="tpu_custom_call" | custom-call | flops 2013265920 | bytes 7864320 | tf_op jit(solution)/shard_map/pallas_call | solution.py:124
  52.3 3.1 %collective-permute-done.8.refs_2_ = bf16[512,1280]{1,0:T(8,128)(2,1)S(1)} collective-permute-done((bf16[512,1280]{1,0:T(8,128)(2,1)}, bf16[512,1280]{1,0:T(8,128)(2,1)S(1)}, u32[]{:S(2)}, u32[]{:S(2)}) %collective-permute-start.8) | collective-permute-done | bytes 1310752 | tf_op jit(solution)/shard_map/ppermute | solution.py:303
  56.9 3.0 %collective-permute-start.13 = (bf16[256,1280]{1,0:T(8,128)(2,1)S(1)}, bf16[256,1280]{1,0:T(8,128)(2,1)S(1)}, u32[]{:S(2)}, u32[]{:S(2)}) collective-permute-start(bf16[256,1280]{1,0:T(8,128)(2,1)S(1)} %slice.91), channel_id=1, source_target_pairs={{0,3},{1,0},{2,1},{3,2},{4,7},{5,4},{6,5},{7,6},{8,11},{9,8},{10,9... | collective-permute-start | bytes 1966088 | tf_op jit(solution)/shard_map/ppermute | solution.py:310
  65.5 6.6 %shard_map.76 = (bf16[384,128]{1,0:T(8,128)(2,1)S(1)}, bf16[384,256]{1,0:T(8,128)(2,1)S(1)}, bf16[384,384]{1,0:T(8,128)(2,1)S(1)}, f32[512,768]{1,0:T(8,128)S(1)}) custom-call(s32[9]{0:T(128)S(1)} %pad_add_fusion.where_ref, bf16[4,3,1280,256]{3,2,1,0:T(8,128)(2,1)S(1)} %copy-done.3, f32[1,768]{1,0:T(1,128)S(1)} %bitcast.95, ...), custom_call_target="tpu_custom_call" | custom-call | flops 4026531840 | bytes 7864320 | tf_op jit(solution)/shard_map/pallas_call | solution.py:124
  77.4 2.9 %shard_map.77 = (bf16[640,128]{1,0:T(8,128)(2,1)S(1)}, bf16[640,256]{1,0:T(8,128)(2,1)S(1)}, bf16[640,384]{1,0:T(8,128)(2,1)S(1)}) custom-call(s32[9]{0:T(128)S(1)} %pad_add_fusion.where_ref, bf16[4,3,1280,256]{3,2,1,0:T(8,128)(2,1)S(1)} %copy-done.3, f32[1,768]{1,0:T(1,128)S(1)} %bitcast.96, bf16[64,5120]{1,0:T(8,128)(2,1)S(1)} %collective-permute-done.10.refs_0_, ...), custom_call_target="tpu_custom_call" | custom-call | flops 2013265920 | bytes 7864320 | tf_op jit(solution)/shard_map/pallas_call | solution.py:124
  80.3 6.3 %collective-permute-done.15.refs_1_ = bf16[768,256]{1,0:T(8,128)(2,1)S(1)} collective-permute-done((bf16[768,256]{1,0:T(8,128)(2,1)S(1)}, bf16[768,256]{1,0:T(8,128)(2,1)S(1)}, u32[]{:S(2)}, u32[]{:S(2)}) %collective-permute-start.15) | collective-permute-done | bytes 393248 | tf_op jit(solution)/shard_map/ppermute | solution.py:317
  90.6 2.9 %collective-permute-start.21 = (bf16[1280,256]{1,0:T(8,128)(2,1)S(1)}, bf16[1280,256]{1,0:T(8,128)(2,1)S(1)}, u32[]{:S(2)}, u32[]{:S(2)}) collective-permute-start(bf16[1280,256]{1,0:T(8,128)(2,1)S(1)} %pad_maximum_fusion.1.refs_5_), channel_id=1, source_target_pairs={{0,24},{4,28},{8,0},{12,4},{16,8},{20,12},{24,16},{28,20},{1,25},{... | collective-permute-start | bytes 1966088 | tf_op jit(solution)/shard_map/ppermute | solution.py:317
  93.5 6.1 %shard_map.78 = (f32[2048,128]{1,0:T(8,128)S(1)}, f32[2048,128]{1,0:T(8,128)S(1)}, f32[2048,128]{1,0:T(8,128)S(1)}) custom-call(bf16[2048,128]{1,0:T(8,128)(2,1)S(1)} %pad_maximum_fusion.4.q_ref, bf16[2048,128]{1,0:T(8,128)(2,1)S(1)} %bitcast.90, bf16[768,256]{1,0:T(8,128)(2,1)S(1)} %pad_maximum_fusion.5.refs_0_, ...), custom_call_target="tpu_custom_call" | custom-call | flops 4831838208 | bytes 1179648 | tf_op jit(solution)/shard_map/pallas_call | solution.py:227
  99.7 6.4 %shard_map.79 = (f32[2048,128]{1,0:T(8,128)S(1)}, f32[2048,128]{1,0:T(8,128)S(1)}, f32[2048,128]{1,0:T(8,128)S(1)}) custom-call(bf16[2048,128]{1,0:T(8,128)(2,1)S(1)} %pad_maximum_fusion.4.q_ref, bf16[2048,128]{1,0:T(8,128)(2,1)S(1)} %bitcast.91, f32[2048,128]{1,0:T(8,128)S(1)} %get-tuple-element.56.refs_0_, f32[2048,128]{1,0:T(8,128)S(1)} %get-tuple-element.57.refs_1_, ...), custom_call_target="tpu_custom_call" | custom-call | flops 4294967296 | bytes 1048576 | tf_op jit(solution)/shard_map/pallas_call | solution.py:227
  106.1 3.3 %collective-permute-done.20.refs_3_ = bf16[1280,256]{1,0:T(8,128)(2,1)S(1)} collective-permute-done((bf16[1280,256]{1,0:T(8,128)(2,1)S(1)}, bf16[1280,256]{1,0:T(8,128)(2,1)S(1)}, u32[]{:S(2)}, u32[]{:S(2)}) %collective-permute-start.20) | collective-permute-done | bytes 655392 | tf_op jit(solution)/shard_map/ppermute | solution.py:317
  109.8 3.2 %collective-permute-start.23 = (bf16[640,256]{1,0:T(8,128)(2,1)S(1)}, bf16[640,256]{1,0:T(8,128)(2,1)S(1)}, u32[]{:S(2)}, u32[]{:S(2)}) collective-permute-start(bf16[640,256]{1,0:T(8,128)(2,1)S(1)} %slice.97), channel_id=1, source_target_pairs={{0,24},{4,28},{8,0},{12,4},{16,8},{20,12},{24,16},{28,20},{1,25},{... | collective-permute-start | bytes 983048 | tf_op jit(solution)/shard_map/ppermute | solution.py:321
  113.0 7.9 %shard_map.80 = (f32[2048,128]{1,0:T(8,128)S(1)}, f32[2048,128]{1,0:T(8,128)S(1)}, f32[2048,128]{1,0:T(8,128)S(1)}) custom-call(bf16[2048,128]{1,0:T(8,128)(2,1)S(1)} %pad_maximum_fusion.4.q_ref, bf16[2048,128]{1,0:T(8,128)(2,1)S(1)} %bitcast.92, f32[2048,128]{1,0:T(8,128)S(1)} %get-tuple-element.60.refs_0_, f32[2048,128]{1,0:T(8,128)S(1)} %get-tuple-element.61.refs_1_, ...), custom_call_target="tpu_custom_call" | custom-call | flops 5368709120 | bytes 1310720 | tf_op jit(solution)/shard_map/pallas_call | solution.py:227
  121.0 4.3 %shard_map.81 = bf16[2048,128]{1,0:T(8,128)(2,1)S(1)} custom-call(bf16[2048,128]{1,0:T(8,128)(2,1)S(1)} %pad_maximum_fusion.4.q_ref, bf16[2048,128]{1,0:T(8,128)(2,1)S(1)} %bitcast.93, f32[2048,128]{1,0:T(8,128)S(1)} %get-tuple-element.63.refs_0_, f32[2048,128]{1,0:T(8,128)S(1)} %get-tuple-element.64.refs_1_, f32[2048,128]{1,0:T(8,128)S(1)} %get-tuple-element.65.refs_2_, ...), custom_call_target="tpu_custom_call" | custom-call | flops 2684354560 | bytes 655360 | tf_op jit(solution)/shard_map/pallas_call | solution.py:227
  130.9 2.5 %collective-permute-done.25.refs_1_ = bf16[256,256]{1,0:T(8,128)(2,1)S(1)} collective-permute-done((bf16[256,256]{1,0:T(8,128)(2,1)S(1)}, bf16[256,256]{1,0:T(8,128)(2,1)S(1)}, u32[]{:S(2)}, u32[]{:S(2)}) %collective-permute-start.25) | collective-permute-done | bytes 131104 | tf_op jit(solution)/shard_map/ppermute | solution.py:351
  136.9 4.0 %copy-done.1 = bf16[4,4,256,1280]{3,2,1,0:T(8,128)(2,1)S(1)} copy-done((bf16[4,4,256,1280]{3,2,1,0:T(8,128)(2,1)S(1)}, bf16[4,4,256,1280]{3,2,1,0:T(8,128)(2,1)}, u32[]{:S(2)}) %copy-start.1) | copy-done | bytes 10485784
  144.6 3.3 %collective-permute-start.30 = (bf16[128,1280]{1,0:T(8,128)(2,1)S(1)}, bf16[128,1280]{1,0:T(8,128)(2,1)S(1)}, u32[]{:S(2)}, u32[]{:S(2)}) collective-permute-start(bf16[128,1280]{1,0:T(8,128)(2,1)S(1)} %get-tuple-element.70), channel_id=1, source_target_pairs={{0,3},{1,0},{2,1},{3,2},{4,7},{5,4},{6,5},{7,6},{8,11},{9,8},{10,9... | collective-permute-start | bytes 983048 | tf_op jit(solution)/shard_map/ppermute | solution.py:358
  147.9 4.3 %collective-permute-done.28 = bf16[128,1280]{1,0:T(8,128)(2,1)S(1)} collective-permute-done((bf16[128,1280]{1,0:T(8,128)(2,1)S(1)}, bf16[128,1280]{1,0:T(8,128)(2,1)S(1)}, u32[]{:S(2)}, u32[]{:S(2)}) %collective-permute-start.28) | collective-permute-done | bytes 327712 | tf_op jit(solution)/shard_map/ppermute | solution.py:357
  153.8 3.8 %collective-permute-start.31 = (bf16[256,1280]{1,0:T(8,128)(2,1)S(1)}, bf16[256,1280]{1,0:T(8,128)(2,1)S(1)}, u32[]{:S(2)}, u32[]{:S(2)}) collective-permute-start(bf16[256,1280]{1,0:T(8,128)(2,1)S(1)} %pad_maximum_fusion.3), channel_id=1, source_target_pairs={{0,3},{1,0},{2,1},{3,2},{4,7},{5,4},{6,5},{7,6},{8,11},{9,8},{10,9... | collective-permute-start | bytes 1966088 | tf_op jit(solution)/shard_map/ppermute | solution.py:363
  159.0 9.3 %collective-permute-done.29 = bf16[256,1280]{1,0:T(8,128)(2,1)S(1)} collective-permute-done((bf16[256,1280]{1,0:T(8,128)(2,1)S(1)}, bf16[256,1280]{1,0:T(8,128)(2,1)S(1)}, u32[]{:S(2)}, u32[]{:S(2)}) %collective-permute-start.29) | collective-permute-done | bytes 655392 | tf_op jit(solution)/shard_map/ppermute | solution.py:362
  (121 shorter events, 61.8 us)
Async XLA Ops:
  1.1 16.5 %collective-permute-start = (bf16[128,1280]{1,0:T(8,128)(2,1)S(1)}, bf16[128,1280]{1,0:T(8,128)(2,1)S(1)}, u32[]{:S(2)}, u32[]{:S(2)}) collective-permute-start(bf16[128,1280]{1,0:T(8,128)(2,1)S(1)} %get-tuple-element.39), channel_id=1, source_target_pairs={{0,32},{32,64},{64,96},{96,0},{1,33},{33,65},{65,97},{97,1},{2,34}... | collective-permute-start | bytes 983048 | tf_op jit(solution)/shard_map/ppermute | solution.py:251
  3.2 16.2 %collective-permute-start.1 = (bf16[128,1280]{1,0:T(8,128)(2,1)S(1)}, bf16[128,1280]{1,0:T(8,128)(2,1)S(1)}, u32[]{:S(2)}, u32[]{:S(2)}) collective-permute-start(bf16[128,1280]{1,0:T(8,128)(2,1)S(1)} %get-tuple-element.39), channel_id=1, source_target_pairs={{0,96},{32,0},{64,32},{96,64},{1,97},{33,1},{65,33},{97,65},{2,98}... | collective-permute-start | bytes 983048 | tf_op jit(solution)/shard_map/ppermute | solution.py:251
  5.4 15.8 %collective-permute-start.2 = (bf16[128,1280]{1,0:T(8,128)(2,1)S(1)}, bf16[128,1280]{1,0:T(8,128)(2,1)S(1)}, u32[]{:S(2)}, u32[]{:S(2)}) collective-permute-start(bf16[128,1280]{1,0:T(8,128)(2,1)S(1)} %get-tuple-element.39), channel_id=1, source_target_pairs={{0,64},{32,96},{64,0},{96,32},{1,65},{33,97},{65,1},{97,33},{2,66}... | collective-permute-start | bytes 983048 | tf_op jit(solution)/shard_map/ppermute | solution.py:251
  7.2 20.3 %collective-permute-start.3 = (bf16[128,1280]{1,0:T(8,128)(2,1)S(1)}, bf16[128,1280]{1,0:T(8,128)(2,1)S(1)}, u32[]{:S(2)}, u32[]{:S(2)}) collective-permute-start(bf16[128,1280]{1,0:T(8,128)(2,1)S(1)} %get-tuple-element.71), channel_id=1, source_target_pairs={{0,1},{1,2},{2,3},{3,0},{4,5},{5,6},{6,7},{7,4},{8,9},{9,10},{10,1... | collective-permute-start | bytes 983048 | tf_op jit(solution)/shard_map/ppermute | solution.py:251
  8.7 18.8 %collective-permute-start.4 = (bf16[128,1280]{1,0:T(8,128)(2,1)S(1)}, bf16[128,1280]{1,0:T(8,128)(2,1)S(1)}, u32[]{:S(2)}, u32[]{:S(2)}) collective-permute-start(bf16[128,1280]{1,0:T(8,128)(2,1)S(1)} %get-tuple-element.71), channel_id=1, source_target_pairs={{0,3},{1,0},{2,1},{3,2},{4,7},{5,4},{6,5},{7,6},{8,11},{9,8},{10,9... | collective-permute-start | bytes 983048 | tf_op jit(solution)/shard_map/ppermute | solution.py:251
  17.6 10.6 %collective-permute-start.5 = (bf16[128,1280]{1,0:T(8,128)(2,1)S(1)}, bf16[128,1280]{1,0:T(8,128)(2,1)S(1)}, u32[]{:S(2)}, u32[]{:S(2)}) collective-permute-start(bf16[128,1280]{1,0:T(8,128)(2,1)S(1)} %get-tuple-element.71), channel_id=1, source_target_pairs={{0,2},{1,3},{2,0},{3,1},{4,6},{5,7},{6,4},{7,5},{8,10},{9,11},{10,... | collective-permute-start | bytes 983048 | tf_op jit(solution)/shard_map/ppermute | solution.py:251
  24.3 31.1 %collective-permute-start.8 = (bf16[512,1280]{1,0:T(8,128)(2,1)}, bf16[512,1280]{1,0:T(8,128)(2,1)S(1)}, u32[]{:S(2)}, u32[]{:S(2)}) collective-permute-start(bf16[512,1280]{1,0:T(8,128)(2,1)} %constant_dynamic-update-slice_fusion.refs_1_), channel_id=1, source_target_pairs={{0,1},{1,2},{2,3},{3,0},{4,5},{5,6},{6,7},{7,4},{8,9},{9,10},{10,1... | collective-permute-start | bytes 3932168 | tf_op jit(solution)/shard_map/ppermute | solution.py:303
  25.8 30.0 %collective-permute-start.9 = (bf16[512,1280]{1,0:T(8,128)(2,1)}, bf16[512,1280]{1,0:T(8,128)(2,1)}, u32[]{:S(2)}, u32[]{:S(2)}) collective-permute-start(bf16[512,1280]{1,0:T(8,128)(2,1)} %constant_dynamic-update-slice_fusion.refs_1_), channel_id=1, source_target_pairs={{0,3},{1,0},{2,1},{3,2},{4,7},{5,4},{6,5},{7,6},{8,11},{9,8},{10,9... | collective-permute-start | bytes 3932168 | tf_op jit(solution)/shard_map/ppermute | solution.py:305
  29.3 30.5 %collective-permute-start.6 = (bf16[128,5120]{1,0:T(8,128)(2,1)S(1)}, bf16[128,5120]{1,0:T(8,128)(2,1)}, u32[]{:S(2)}, u32[]{:S(2)}) collective-permute-start(bf16[128,5120]{1,0:T(8,128)(2,1)S(1)} %pad_maximum_fusion.refs_0_), channel_id=1, source_target_pairs={{0,32},{32,64},{64,96},{96,0},{1,33},{33,65},{65,97},{97,1},{2,34}... | collective-permute-start | bytes 3932168 | tf_op jit(solution)/shard_map/ppermute | solution.py:302
  30.6 31.5 %collective-permute-start.7 = (bf16[128,5120]{1,0:T(8,128)(2,1)S(1)}, bf16[128,5120]{1,0:T(8,128)(2,1)}, u32[]{:S(2)}, u32[]{:S(2)}) collective-permute-start(bf16[128,5120]{1,0:T(8,128)(2,1)S(1)} %pad_maximum_fusion.refs_0_), channel_id=1, source_target_pairs={{0,96},{32,0},{64,32},{96,64},{1,97},{33,1},{65,33},{97,65},{2,98}... | collective-permute-start | bytes 3932168 | tf_op jit(solution)/shard_map/ppermute | solution.py:304
  55.4 20.4 %collective-permute-start.12 = (bf16[256,1280]{1,0:T(8,128)(2,1)S(1)}, bf16[256,1280]{1,0:T(8,128)(2,1)S(1)}, u32[]{:S(2)}, u32[]{:S(2)}) collective-permute-start(bf16[256,1280]{1,0:T(8,128)(2,1)S(1)} %slice.90), channel_id=1, source_target_pairs={{0,1},{1,2},{2,3},{3,0},{4,5},{5,6},{6,7},{7,4},{8,9},{9,10},{10,1... | collective-permute-start | bytes 1966088 | tf_op jit(solution)/shard_map/ppermute | solution.py:309
  56.9 20.5 %collective-permute-start.13 = (bf16[256,1280]{1,0:T(8,128)(2,1)S(1)}, bf16[256,1280]{1,0:T(8,128)(2,1)S(1)}, u32[]{:S(2)}, u32[]{:S(2)}) collective-permute-start(bf16[256,1280]{1,0:T(8,128)(2,1)S(1)} %slice.91), channel_id=1, source_target_pairs={{0,3},{1,0},{2,1},{3,2},{4,7},{5,4},{6,5},{7,6},{8,11},{9,8},{10,9... | collective-permute-start | bytes 1966088 | tf_op jit(solution)/shard_map/ppermute | solution.py:310
  61.0 16.4 %collective-permute-start.10 = (bf16[64,5120]{1,0:T(8,128)(2,1)S(1)}, bf16[64,5120]{1,0:T(8,128)(2,1)S(1)}, u32[]{:S(2)}, u32[]{:S(2)}) collective-permute-start(bf16[64,5120]{1,0:T(8,128)(2,1)S(1)} %slice.88), channel_id=1, source_target_pairs={{0,32},{32,64},{64,96},{96,0},{1,33},{33,65},{65,97},{97,1},{2,34}... | collective-permute-start | bytes 1966088 | tf_op jit(solution)/shard_map/ppermute | solution.py:307
  63.2 14.2 %collective-permute-start.11 = (bf16[64,5120]{1,0:T(8,128)(2,1)S(1)}, bf16[64,5120]{1,0:T(8,128)(2,1)S(1)}, u32[]{:S(2)}, u32[]{:S(2)}) collective-permute-start(bf16[64,5120]{1,0:T(8,128)(2,1)S(1)} %slice.89), channel_id=1, source_target_pairs={{0,96},{32,0},{64,32},{96,64},{1,97},{33,1},{65,33},{97,65},{2,98}... | collective-permute-start | bytes 1966088 | tf_op jit(solution)/shard_map/ppermute | solution.py:308
  73.9 12.7 %collective-permute-start.15 = (bf16[768,256]{1,0:T(8,128)(2,1)S(1)}, bf16[768,256]{1,0:T(8,128)(2,1)S(1)}, u32[]{:S(2)}, u32[]{:S(2)}) collective-permute-start(bf16[768,256]{1,0:T(8,128)(2,1)S(1)} %pad_maximum_fusion.5.refs_0_), channel_id=1, source_target_pairs={{0,8},{4,12},{8,16},{12,20},{16,24},{20,28},{24,0},{28,4},{1,9},{5... | collective-permute-start | bytes 1179656 | tf_op jit(solution)/shard_map/ppermute | solution.py:317
  75.7 10.9 %collective-permute-start.16 = (bf16[768,256]{1,0:T(8,128)(2,1)S(1)}, bf16[768,256]{1,0:T(8,128)(2,1)S(1)}, u32[]{:S(2)}, u32[]{:S(2)}) collective-permute-start(bf16[768,256]{1,0:T(8,128)(2,1)S(1)} %pad_maximum_fusion.5.refs_0_), channel_id=1, source_target_pairs={{0,24},{4,28},{8,0},{12,4},{16,8},{20,12},{24,16},{28,20},{1,25},{... | collective-permute-start | bytes 1179656 | tf_op jit(solution)/shard_map/ppermute | solution.py:317
  86.6 13.0 %collective-permute-start.18 = (bf16[384,256]{1,0:T(8,128)(2,1)S(1)}, bf16[384,256]{1,0:T(8,128)(2,1)S(1)}, u32[]{:S(2)}, u32[]{:S(2)}) collective-permute-start(bf16[384,256]{1,0:T(8,128)(2,1)S(1)} %slice.73), channel_id=1, source_target_pairs={{0,8},{4,12},{8,16},{12,20},{16,24},{20,28},{24,0},{28,4},{1,9},{5... | collective-permute-start | bytes 589832 | tf_op jit(solution)/shard_map/ppermute | solution.py:321
  88.3 11.4 %collective-permute-start.19 = (bf16[384,256]{1,0:T(8,128)(2,1)S(1)}, bf16[384,256]{1,0:T(8,128)(2,1)S(1)}, u32[]{:S(2)}, u32[]{:S(2)}) collective-permute-start(bf16[384,256]{1,0:T(8,128)(2,1)S(1)} %slice.74), channel_id=1, source_target_pairs={{0,24},{4,28},{8,0},{12,4},{16,8},{20,12},{24,16},{28,20},{1,25},{... | collective-permute-start | bytes 589832 | tf_op jit(solution)/shard_map/ppermute | solution.py:321
  90.1 19.2 %collective-permute-start.20 = (bf16[1280,256]{1,0:T(8,128)(2,1)S(1)}, bf16[1280,256]{1,0:T(8,128)(2,1)S(1)}, u32[]{:S(2)}, u32[]{:S(2)}) collective-permute-start(bf16[1280,256]{1,0:T(8,128)(2,1)S(1)} %pad_maximum_fusion.1.refs_5_), channel_id=1, source_target_pairs={{0,8},{4,12},{8,16},{12,20},{16,24},{20,28},{24,0},{28,4},{1,9},{5... | collective-permute-start | bytes 1966088 | tf_op jit(solution)/shard_map/ppermute | solution.py:317
  90.6 19.2 %collective-permute-start.21 = (bf16[1280,256]{1,0:T(8,128)(2,1)S(1)}, bf16[1280,256]{1,0:T(8,128)(2,1)S(1)}, u32[]{:S(2)}, u32[]{:S(2)}) collective-permute-start(bf16[1280,256]{1,0:T(8,128)(2,1)S(1)} %pad_maximum_fusion.1.refs_5_), channel_id=1, source_target_pairs={{0,24},{4,28},{8,0},{12,4},{16,8},{20,12},{24,16},{28,20},{1,25},{... | collective-permute-start | bytes 1966088 | tf_op jit(solution)/shard_map/ppermute | solution.py:317
  109.4 11.6 %collective-permute-start.22 = (bf16[640,256]{1,0:T(8,128)(2,1)S(1)}, bf16[640,256]{1,0:T(8,128)(2,1)S(1)}, u32[]{:S(2)}, u32[]{:S(2)}) collective-permute-start(bf16[640,256]{1,0:T(8,128)(2,1)S(1)} %slice.96), channel_id=1, source_target_pairs={{0,8},{4,12},{8,16},{12,20},{16,24},{20,28},{24,0},{28,4},{1,9},{5... | collective-permute-start | bytes 983048 | tf_op jit(solution)/shard_map/ppermute | solution.py:321
  109.8 11.2 %collective-permute-start.23 = (bf16[640,256]{1,0:T(8,128)(2,1)S(1)}, bf16[640,256]{1,0:T(8,128)(2,1)S(1)}, u32[]{:S(2)}, u32[]{:S(2)}) collective-permute-start(bf16[640,256]{1,0:T(8,128)(2,1)S(1)} %slice.97), channel_id=1, source_target_pairs={{0,24},{4,28},{8,0},{12,4},{16,8},{20,12},{24,16},{28,20},{1,25},{... | collective-permute-start | bytes 983048 | tf_op jit(solution)/shard_map/ppermute | solution.py:321
  152.3 16.0 %collective-permute-start.29 = (bf16[256,1280]{1,0:T(8,128)(2,1)S(1)}, bf16[256,1280]{1,0:T(8,128)(2,1)S(1)}, u32[]{:S(2)}, u32[]{:S(2)}) collective-permute-start(bf16[256,1280]{1,0:T(8,128)(2,1)S(1)} %pad_maximum_fusion.2), channel_id=1, source_target_pairs={{0,1},{1,2},{2,3},{3,0},{4,5},{5,6},{6,7},{7,4},{8,9},{9,10},{10,1... | collective-permute-start | bytes 1966088 | tf_op jit(solution)/shard_map/ppermute | solution.py:362
  153.8 15.7 %collective-permute-start.31 = (bf16[256,1280]{1,0:T(8,128)(2,1)S(1)}, bf16[256,1280]{1,0:T(8,128)(2,1)S(1)}, u32[]{:S(2)}, u32[]{:S(2)}) collective-permute-start(bf16[256,1280]{1,0:T(8,128)(2,1)S(1)} %pad_maximum_fusion.3), channel_id=1, source_target_pairs={{0,3},{1,0},{2,1},{3,2},{4,7},{5,4},{6,5},{7,6},{8,11},{9,8},{10,9... | collective-permute-start | bytes 1966088 | tf_op jit(solution)/shard_map/ppermute | solution.py:363
  (20 other events, 135.0 us)
where the time goes:
time: 172 us; the launch traced here: 171 us
  Pallas kernels  51.3 us (30%)
  starting transfers between devices  49.4 us (29%)
  waiting for transfers between devices  39.8 us (23%)
  local copies, waits for them, and re-layouts  24.2 us (14%)
  between operations  2.96 us (2%)
  other arithmetic  2.68 us (2%)
    pallas_call x4, Pallas kernels, attention(): pl.pallas_call(functools.partial(attn_kernel, sizes, first_block, begin,...  24.7 us
    unnamed x27, local copies, waits for them, and re-layouts  17.5 us
    pallas_call x3, Pallas kernels, project_stage(): pl.pallas_call(functools.partial(stage_kernel, len(a_parts), b_slices, in...  13.1 us
    ppermute x6, starting transfers between devices, direct(): return [value] + [pp(value, axis, ring(n, s)) for s in (1, -1, 2)]  11.1 us
    ppermute x4, waiting for transfers between devices, near_y(): return [pp(kv, 'blk', y_ring(nb, s)) for s in (1, -1)]  9.56 us
    ppermute x1, waiting for transfers between devices, local(): from_m = pp(to_p, 'tensor', ring(nt, 1))  9.34 us
    pallas_call x2, Pallas kernels, load(): pl.pallas_call(functools.partial(load_kernel, pick), in_specs=[pl.BlockSp...  8.56 us
    ppermute x4, starting transfers between devices, near_y(): return [pp(kv, 'blk', y_ring(nb, s)) for s in (1, -1)]  6.79 us
  transfers between devices with their start and end apart: 32, of which 13 were waited for; matrix products, arithmetic and copies ran while one was open for 6% of the time, Pallas kernels for 27%

commit v1 on v0

--- a/solution.py
+++ b/solution.py
@@ -50,25 +50,27 @@
     return [jax.ShapeDtypeStruct((rows, n * HD), jnp.bfloat16) for n in (1, 2, 3)]
 
 
-def load_kernel(pick, where_ref, hbm, o_ref, sems):
+def load_kernel(where_ref, x_ref, hbm, o_ref, sems):
+    width = o_ref.shape[3]
     copies = []
-    for i in range(o_ref.shape[0]):
-        copies.append(pltpu.make_async_copy(pick(hbm, where_ref[i]), o_ref.at[i], sems.at[i]))
+    for i in range(4):
+        cols = pl.ds(pl.multiple_of(where_ref[i] * width, width), width)
+        copies.append(pltpu.make_async_copy(hbm.at[:, :, cols], o_ref.at[i], sems.at[i]))
         copies[-1].start()
     for copy in copies:
         copy.wait()
 
 
-def load(where, w, shape, pick, limit):
+def load_columns(where, w, x):
     return pl.pallas_call(
-        functools.partial(load_kernel, pick),
-        in_specs=[pl.BlockSpec(memory_space=pltpu.SMEM), pl.BlockSpec(memory_space=pltpu.HBM)],
+        load_kernel,
+        in_specs=[pl.BlockSpec(memory_space=pltpu.SMEM), VM, pl.BlockSpec(memory_space=pltpu.HBM)],
         out_specs=VM,
-        out_shape=jax.ShapeDtypeStruct((4,) + shape, w.dtype),
+        out_shape=jax.ShapeDtypeStruct((4,) + w.shape[:2] + (w.shape[2] // 4,), w.dtype),
         scratch_shapes=[pltpu.SemaphoreType.DMA((4,))],
-        compiler_params=pltpu.CompilerParams(vmem_limit_bytes=limit << 20),
+        compiler_params=pltpu.CompilerParams(vmem_limit_bytes=40 << 20),
         cost_estimate=pl.CostEstimate(flops=0, bytes_accessed=w.size * 4, transcendentals=0),
-    )(where, w)
+    )(where, x, w)
 
 
 def stage_kernel(n_a, b_slices, n_done, has_part, emit_all, where_ref, w_ref, scale_ref, *refs):
@@ -77,17 +79,18 @@
     done_refs, refs = refs[:n_done], refs[n_done:]
     part_refs, refs = refs[:has_part], refs[has_part:]
     outs, acc_ref = refs[:-1], refs[-1]
-    feat = w_ref.shape[2]
+    feat = w_ref.shape[1] // 4
     na = sum(r.shape[0] for r in a_refs)
     fresh = not has_part
     for i in range(4):
+        at = pl.ds(pl.multiple_of(where_ref[i] * feat, feat), feat)
         x = [r[:, i * feat : (i + 1) * feat] for r in a_refs]
         x += [r[...] for r, s in zip(b_refs, b_slices) if s == i]
         with_b = len(x) > n_a
         x = jnp.concatenate(x, axis=0) if len(x) > 1 else x[0]
         for c in range(3):
             cols = slice(c * 256, (c + 1) * 256)
-            d = jnp.dot(x, w_ref[i, c], preferred_element_type=jnp.float32)
+            d = jnp.dot(x, w_ref[c, at, :], preferred_element_type=jnp.float32)
             acc_ref[:na, cols] = d[:na] if i == 0 else acc_ref[:na, cols] + d[:na]
             if with_b:
                 first = i == min(b_slices)
@@ -110,7 +113,7 @@
 
 
 def project_stage(where, w, scale, a_parts, b_parts, b_slices, done, part, emit_all):
-    feat = w.shape[2]
+    feat = w.shape[1] // 4
     na = sum(x.shape[0] for x in a_parts)
     nb = 512 if part is None else part.shape[0]
     f32 = lambda n: jax.ShapeDtypeStruct((n, 768), jnp.float32)
@@ -251,17 +254,8 @@
         return [value] + [pp(value, axis, ring(n, s)) for s in (1, -1, 2)]
 
     where = jnp.concatenate([(t + offsets) % nt, core[None], (u - offsets) % nu])
-    feat = tokens.shape[1]
-
-    def at_rows(ref, i):
-        return ref.at[:, pl.ds(pl.multiple_of(i * feat, feat), feat), :]
-
-    def at_cols(ref, i):
-        return ref.at[:, :, pl.ds(pl.multiple_of(i * feat, feat), feat)]
-
+    w = jnp.transpose(w_qkv, (1, 0, 2))
     hold = lax.optimization_barrier
-    w = load(where, jnp.transpose(w_qkv, (1, 0, 2)), (3, feat, w_qkv.shape[2]), at_rows, 46)
-    w_o = load(where, w_out, w_out.shape[:2] + (feat,), at_cols, 34)
     scale = qkv_scale * jnp.array([LOG2E / math.sqrt(HD), 1.0, 1.0], jnp.float32)[:, None]
     scale = jnp.repeat(scale.reshape(1, 6), HD, axis=1)
 
@@ -297,8 +291,7 @@
     bias = jnp.repeat(bias, BLOCK, axis=0)
 
     a_own = jnp.concatenate(direct(tokens[:half], "tensor", nt), axis=1)
-    b_parts, w = hold((direct(tokens[half:], "ulysses", nu), w))
-    b_own = jnp.concatenate(b_parts, axis=0)
+    b_own = jnp.concatenate(direct(tokens[half:], "ulysses", nu), axis=0)
     a_m = pp(a_own, "ulysses", ring(nu, 1))
     b_m = pp(b_own, "tensor", ring(nt, 1))
     a_p = pp(a_own, "ulysses", ring(nu, -1))
@@ -321,7 +314,7 @@
         return [pp(kv_m[:h], "blk", y_ring(nb, 1)), pp(kv_p[h:], "blk", y_ring(nb, -1))]
 
     done, part = project_stage(where, w, scale, [a_own], [b_own], (0,), None, None, False)
-    done, bias, w_o = hold((done, bias, w_o))
+    done, bias = hold((done, bias))
     q1, kv1, give1, part = project_stage(
         where, w, scale, [a_m, a_p], [b_m, b_p], (1, 2), done, part, False
     )
@@ -350,6 +343,7 @@
     arrived = [heads[0]] + [
         pp(heads[i], "ulysses", ring(nu, OFFSETS[i])) for i in range(1, nu)
     ]
+    w_o = load_columns(where, w_out, heads[0])
     bf = jnp.bfloat16
     far_0, far_1 = out_project(where, arrived, w_o, (3,), bf, 2)
     rows = 2 * half

time: 172 us -> 170 us (0.988)
  waiting for transfers between devices: 39.8 us -> 56.7 us
  local copies, waits for them, and re-layouts: 24.2 us -> 11.1 us
  Pallas kernels: 51.3 us -> 46.7 us
    unnamed x27 -> x18, local copies, waits for them, and re-layouts: 17.5 us -> 4.07 us
    ppermute x1, waiting for transfers between devices: 0.01 us -> 13.3 us  [local(): a_m = pp(a_own, 'ulysses', ring(nu, 1))]
    ppermute x1, waiting for transfers between devices: 1.2 us -> 9.56 us  [local(): from_p = pp(to_m, 'tensor', ring(nt, -1))]
    ppermute x6, waiting for transfers between devices: 1.84 us -> 6.62 us  [direct(): return [value] + [pp(value, axis, ring(n, s)) for s in (1, -1, 2)]]
    ppermute x1, waiting for transfers between devices: 9.34 us -> 4.69 us  [local(): from_m = pp(to_p, 'tensor', ring(nt, 1))]
    pallas_call x2 -> x1, Pallas kernels: 8.56 us -> 4.66 us  [load_columns(): pl.pallas_call(load_kernel, in_specs=[pl.BlockSpec(memory_space=pltpu.SME...]
    ppermute x1, waiting for transfers between devices: 1.28 us -> 4.58 us  [local(): far_p = pp(far_1, 'tensor', ring(nt, -1))]
    ppermute x1, starting transfers between devices: 3.29 us -> 0.09 us  [local(): far_p = pp(far_1, 'tensor', ring(nt, -1))]
  transfers between devices with their start and end apart: 32 -> 32, of which waited for: 13 -> 15; matrix products, arithmetic and copies ran while one was open for 6% -> 5% of each run, Pallas kernels for 27% -> 24%
where the time goes in v1:
time: 170 us; the launch traced here: 169 us
  waiting for transfers between devices  56.7 us (33%)
  starting transfers between devices  47.8 us (28%)
  Pallas kernels  46.7 us (27%)
  local copies, waits for them, and re-layouts  11.1 us (7%)
  other arithmetic  3.77 us (2%)
  between operations  3.12 us (2%)
    pallas_call x4, Pallas kernels, attention(): pl.pallas_call(functools.partial(attn_kernel, sizes, first_block, begin,...  24.4 us
    ppermute x1, waiting for transfers between devices, local(): a_m = pp(a_own, 'ulysses', ring(nu, 1))  13.3 us
    pallas_call x3, Pallas kernels, project_stage(): pl.pallas_call(functools.partial(stage_kernel, len(a_parts), b_slices, in...  12.7 us
    ppermute x6, starting transfers between devices, direct(): return [value] + [pp(value, axis, ring(n, s)) for s in (1, -1, 2)]  11.8 us
    ppermute x1, waiting for transfers between devices, local(): from_p = pp(to_m, 'tensor', ring(nt, -1))  9.56 us
    ppermute x4, waiting for transfers between devices, near_y(): return [pp(kv, 'blk', y_ring(nb, s)) for s in (1, -1)]  8.68 us
    ppermute x4, starting transfers between devices, near_y(): return [pp(kv, 'blk', y_ring(nb, s)) for s in (1, -1)]  6.66 us
    ppermute x6, waiting for transfers between devices, direct(): return [value] + [pp(value, axis, ring(n, s)) for s in (1, -1, 2)]  6.62 us
  transfers between devices with their start and end apart: 32, of which 15 were waited for; matrix products, arithmetic and copies ran while one was open for 5% of the time, Pallas kernels for 24%

profile of v1, /device:TPU:0, one launch (start us, length us, event | category | flops | bytes accessed | tf_op | source)
XLA Modules:
  0.0 169.5 jit_solution(15730446895657166293)
XLA Ops:
  1.1 3.2 %collective-permute-start.2 = (bf16[128,1280]{1,0:T(8,128)(2,1)S(1)}, bf16[128,1280]{1,0:T(8,128)(2,1)S(1)}, u32[]{:S(2)}, u32[]{:S(2)}) collective-permute-start(bf16[128,1280]{1,0:T(8,128)(2,1)S(1)} %get-tuple-element.60), channel_id=1, source_target_pairs={{0,2},{1,3},{2,0},{3,1},{4,6},{5,7},{6,4},{7,5},{8,10},{9,11},{10,... | collective-permute-start | bytes 983048 | tf_op jit(solution)/shard_map/ppermute | solution.py:254
  6.3 3.9 %collective-permute-start.7 = (bf16[128,1280]{1,0:T(8,128)(2,1)S(1)}, bf16[128,1280]{1,0:T(8,128)(2,1)S(1)}, u32[]{:S(2)}, u32[]{:S(2)}) collective-permute-start(bf16[128,1280]{1,0:T(8,128)(2,1)S(1)} %get-tuple-element.59), channel_id=1, source_target_pairs={{0,64},{32,96},{64,0},{96,32},{1,65},{33,97},{65,1},{97,33},{2,66}... | collective-permute-start | bytes 983048 | tf_op jit(solution)/shard_map/ppermute | solution.py:254
  11.0 2.4 %collective-permute-done.2 = bf16[128,1280]{1,0:T(8,128)(2,1)S(1)} collective-permute-done((bf16[128,1280]{1,0:T(8,128)(2,1)S(1)}, bf16[128,1280]{1,0:T(8,128)(2,1)S(1)}, u32[]{:S(2)}, u32[]{:S(2)}) %collective-permute-start.2) | collective-permute-done | bytes 327712 | tf_op jit(solution)/shard_map/ppermute | solution.py:254
  15.4 4.0 %collective-permute-done.1 = bf16[128,1280]{1,0:T(8,128)(2,1)S(1)} collective-permute-done((bf16[128,1280]{1,0:T(8,128)(2,1)S(1)}, bf16[128,1280]{1,0:T(8,128)(2,1)S(1)}, u32[]{:S(2)}, u32[]{:S(2)}) %collective-permute-start.1) | collective-permute-done | bytes 327712 | tf_op jit(solution)/shard_map/ppermute | solution.py:254
  22.5 2.2 %collective-permute-start.4 = (bf16[128,5120]{1,0:T(8,128)(2,1)S(1)}, bf16[128,5120]{1,0:T(8,128)(2,1)}, u32[]{:S(2)}, u32[]{:S(2)}) collective-permute-start(bf16[128,5120]{1,0:T(8,128)(2,1)S(1)} %pad_maximum_fusion.refs_0_), channel_id=1, source_target_pairs={{0,96},{32,0},{64,32},{96,64},{1,97},{33,1},{65,33},{97,65},{2,98}... | collective-permute-start | bytes 3932168 | tf_op jit(solution)/shard_map/ppermute | solution.py:297
  34.3 3.2 %copy-done = bf16[5120,3,256]{2,0,1:T(8,128)(2,1)S(1)} copy-done((bf16[5120,3,256]{2,0,1:T(8,128)(2,1)S(1)}, bf16[5120,3,256]{2,0,1:T(8,128)(2,1)}, u32[]{:S(2)}) %copy-start) | copy-done | bytes 7864344
  37.5 2.8 %shard_map.73 = (f32[128,768]{1,0:T(8,128)S(1)}, f32[512,768]{1,0:T(8,128)S(1)}) custom-call(s32[9]{0:T(128)S(1)} %pad_add_fusion.where_ref, bf16[3,5120,256]{2,1,0:T(8,128)(2,1)S(1)} %bitcast.87, f32[1,768]{1,0:T(1,128)S(1)} %bitcast.98, bf16[128,5120]{1,0:T(8,128)(2,1)S(1)} %pad_maximum_fusion.refs_0_, bf16[512,1280]{1,0:T(8,128)(2,1)S(1)} %pad_maximum_fusion.1.refs_1_), custom_call_target="tpu_custom_call" | custom-call | flops 2013265920 | bytes 7864320 | tf_op jit(solution)/shard_map/pallas_call | solution.py:127
  40.4 13.3 %collective-permute-done.3.refs_0_ = bf16[128,5120]{1,0:T(8,128)(2,1)} collective-permute-done((bf16[128,5120]{1,0:T(8,128)(2,1)S(1)}, bf16[128,5120]{1,0:T(8,128)(2,1)}, u32[]{:S(2)}, u32[]{:S(2)}) %collective-permute-start.3) | collective-permute-done | bytes 1310752 | tf_op jit(solution)/shard_map/ppermute | solution.py:295
  56.4 3.0 %collective-permute-start.11 = (bf16[64,5120]{1,0:T(8,128)(2,1)S(1)}, bf16[64,5120]{1,0:T(8,128)(2,1)S(1)}, u32[]{:S(2)}, u32[]{:S(2)}) collective-permute-start(bf16[64,5120]{1,0:T(8,128)(2,1)S(1)} %slice.89), channel_id=1, source_target_pairs={{0,96},{32,0},{64,32},{96,64},{1,97},{33,1},{65,33},{97,65},{2,98}... | collective-permute-start | bytes 1966088 | tf_op jit(solution)/shard_map/ppermute | solution.py:301
  65.0 7.0 %shard_map.74 = (bf16[384,128]{1,0:T(8,128)(2,1)S(1)}, bf16[384,256]{1,0:T(8,128)(2,1)S(1)}, bf16[384,384]{1,0:T(8,128)(2,1)S(1)}, f32[512,768]{1,0:T(8,128)S(1)}) custom-call(s32[9]{0:T(128)S(1)} %pad_add_fusion.where_ref, bf16[3,5120,256]{2,1,0:T(8,128)(2,1)S(1)} %bitcast.88, f32[1,768]{1,0:T(1,128)S(1)} %bitcast.99, ...), custom_call_target="tpu_custom_call" | custom-call | flops 4026531840 | bytes 7864320 | tf_op jit(solution)/shard_map/pallas_call | solution.py:127
  78.5 2.9 %shard_map.75 = (bf16[640,128]{1,0:T(8,128)(2,1)S(1)}, bf16[640,256]{1,0:T(8,128)(2,1)S(1)}, bf16[640,384]{1,0:T(8,128)(2,1)S(1)}) custom-call(s32[9]{0:T(128)S(1)} %pad_add_fusion.where_ref, bf16[3,5120,256]{2,1,0:T(8,128)(2,1)S(1)} %bitcast.89, f32[1,768]{1,0:T(1,128)S(1)} %bitcast.100, bf16[64,5120]{1,0:T(8,128)(2,1)S(1)} %collective-permute-done.10.refs_0_, ...), custom_call_target="tpu_custom_call" | custom-call | flops 2013265920 | bytes 7864320 | tf_op jit(solution)/shard_map/pallas_call | solution.py:127
  81.4 4.9 %collective-permute-done.15.refs_1_ = bf16[768,256]{1,0:T(8,128)(2,1)S(1)} collective-permute-done((bf16[768,256]{1,0:T(8,128)(2,1)S(1)}, bf16[768,256]{1,0:T(8,128)(2,1)S(1)}, u32[]{:S(2)}, u32[]{:S(2)}) %collective-permute-start.15) | collective-permute-done | bytes 393248 | tf_op jit(solution)/shard_map/ppermute | solution.py:310
  90.2 2.9 %collective-permute-start.21 = (bf16[1280,256]{1,0:T(8,128)(2,1)S(1)}, bf16[1280,256]{1,0:T(8,128)(2,1)S(1)}, u32[]{:S(2)}, u32[]{:S(2)}) collective-permute-start(bf16[1280,256]{1,0:T(8,128)(2,1)S(1)} %pad_maximum_fusion.2.refs_5_), channel_id=1, source_target_pairs={{0,24},{4,28},{8,0},{12,4},{16,8},{20,12},{24,16},{28,20},{1,25},{... | collective-permute-start | bytes 1966088 | tf_op jit(solution)/shard_map/ppermute | solution.py:310
  93.2 5.9 %shard_map.76 = (f32[2048,128]{1,0:T(8,128)S(1)}, f32[2048,128]{1,0:T(8,128)S(1)}, f32[2048,128]{1,0:T(8,128)S(1)}) custom-call(bf16[2048,128]{1,0:T(8,128)(2,1)S(1)} %pad_maximum_fusion.5.q_ref, bf16[2048,128]{1,0:T(8,128)(2,1)S(1)} %bitcast.94, bf16[768,256]{1,0:T(8,128)(2,1)S(1)} %pad_maximum_fusion.6.refs_0_, ...), custom_call_target="tpu_custom_call" | custom-call | flops 4831838208 | bytes 1179648 | tf_op jit(solution)/shard_map/pallas_call | solution.py:230
  99.1 6.3 %shard_map.77 = (f32[2048,128]{1,0:T(8,128)S(1)}, f32[2048,128]{1,0:T(8,128)S(1)}, f32[2048,128]{1,0:T(8,128)S(1)}) custom-call(bf16[2048,128]{1,0:T(8,128)(2,1)S(1)} %pad_maximum_fusion.5.q_ref, bf16[2048,128]{1,0:T(8,128)(2,1)S(1)} %bitcast.95, f32[2048,128]{1,0:T(8,128)S(1)} %get-tuple-element.45.refs_0_, f32[2048,128]{1,0:T(8,128)S(1)} %get-tuple-element.46.refs_1_, ...), custom_call_target="tpu_custom_call" | custom-call | flops 4294967296 | bytes 1048576 | tf_op jit(solution)/shard_map/pallas_call | solution.py:230
  105.4 3.8 %collective-permute-done.20.refs_3_ = bf16[1280,256]{1,0:T(8,128)(2,1)S(1)} collective-permute-done((bf16[1280,256]{1,0:T(8,128)(2,1)S(1)}, bf16[1280,256]{1,0:T(8,128)(2,1)S(1)}, u32[]{:S(2)}, u32[]{:S(2)}) %collective-permute-start.20) | collective-permute-done | bytes 655392 | tf_op jit(solution)/shard_map/ppermute | solution.py:310
  109.4 3.4 %collective-permute-start.23 = (bf16[640,256]{1,0:T(8,128)(2,1)S(1)}, bf16[640,256]{1,0:T(8,128)(2,1)S(1)}, u32[]{:S(2)}, u32[]{:S(2)}) collective-permute-start(bf16[640,256]{1,0:T(8,128)(2,1)S(1)} %slice.97), channel_id=1, source_target_pairs={{0,24},{4,28},{8,0},{12,4},{16,8},{20,12},{24,16},{28,20},{1,25},{... | collective-permute-start | bytes 983048 | tf_op jit(solution)/shard_map/ppermute | solution.py:314
  112.9 7.9 %shard_map.78 = (f32[2048,128]{1,0:T(8,128)S(1)}, f32[2048,128]{1,0:T(8,128)S(1)}, f32[2048,128]{1,0:T(8,128)S(1)}) custom-call(bf16[2048,128]{1,0:T(8,128)(2,1)S(1)} %pad_maximum_fusion.5.q_ref, bf16[2048,128]{1,0:T(8,128)(2,1)S(1)} %bitcast.96, f32[2048,128]{1,0:T(8,128)S(1)} %get-tuple-element.49.refs_0_, f32[2048,128]{1,0:T(8,128)S(1)} %get-tuple-element.50.refs_1_, ...), custom_call_target="tpu_custom_call" | custom-call | flops 5368709120 | bytes 1310720 | tf_op jit(solution)/shard_map/pallas_call | solution.py:230
  120.8 4.3 %shard_map.79 = bf16[2048,128]{1,0:T(8,128)(2,1)S(1)} custom-call(bf16[2048,128]{1,0:T(8,128)(2,1)S(1)} %pad_maximum_fusion.5.q_ref, bf16[2048,128]{1,0:T(8,128)(2,1)S(1)} %bitcast.97, f32[2048,128]{1,0:T(8,128)S(1)} %get-tuple-element.52.refs_0_, f32[2048,128]{1,0:T(8,128)S(1)} %get-tuple-element.53.refs_1_, f32[2048,128]{1,0:T(8,128)S(1)} %get-tuple-element.54.refs_2_, ...), custom_call_target="tpu_custom_call" | custom-call | flops 2684354560 | bytes 655360 | tf_op jit(solution)/shard_map/pallas_call | solution.py:230
  130.5 4.7 %shard_map.80.refs_4_ = bf16[4,4,256,1280]{3,2,1,0:T(8,128)(2,1)S(1)} custom-call(s32[9]{0:T(128)S(1)} %pad_add_fusion.where_ref, bf16[256,256]{1,0:T(8,128)(2,1)S(1)} %bitcast.90, bf16[4,256,5120]{2,1,0:T(8,128)(2,1)} %hbm.1), custom_call_target="tpu_custom_call" | custom-call | bytes 20971520 | tf_op jit(solution)/shard_map/pallas_call | solution.py:65
  135.2 3.0 %collective-permute-done.26.refs_2_ = bf16[256,256]{1,0:T(8,128)(2,1)S(1)} collective-permute-done((bf16[256,256]{1,0:T(8,128)(2,1)S(1)}, bf16[256,256]{1,0:T(8,128)(2,1)S(1)}, u32[]{:S(2)}, u32[]{:S(2)}) %collective-permute-start.26) | collective-permute-done | bytes 131104 | tf_op jit(solution)/shard_map/ppermute | solution.py:344
  144.0 4.6 %collective-permute-done.30 = bf16[128,1280]{1,0:T(8,128)(2,1)S(1)} collective-permute-done((bf16[128,1280]{1,0:T(8,128)(2,1)S(1)}, bf16[128,1280]{1,0:T(8,128)(2,1)S(1)}, u32[]{:S(2)}, u32[]{:S(2)}) %collective-permute-start.30) | collective-permute-done | bytes 327712 | tf_op jit(solution)/shard_map/ppermute | solution.py:352
  154.1 9.6 %collective-permute-done.31 = bf16[256,1280]{1,0:T(8,128)(2,1)S(1)} collective-permute-done((bf16[256,1280]{1,0:T(8,128)(2,1)S(1)}, bf16[256,1280]{1,0:T(8,128)(2,1)S(1)}, u32[]{:S(2)}, u32[]{:S(2)}) %collective-permute-start.31) | collective-permute-done | bytes 655392 | tf_op jit(solution)/shard_map/ppermute | solution.py:357
  163.7 4.7 %collective-permute-done.29 = bf16[256,1280]{1,0:T(8,128)(2,1)S(1)} collective-permute-done((bf16[256,1280]{1,0:T(8,128)(2,1)S(1)}, bf16[256,1280]{1,0:T(8,128)(2,1)S(1)}, u32[]{:S(2)}, u32[]{:S(2)}) %collective-permute-start.29) | collective-permute-done | bytes 655392 | tf_op jit(solution)/shard_map/ppermute | solution.py:356
  (111 shorter events, 52.5 us)
Async XLA Ops:
  1.1 12.2 %collective-permute-start.2 = (bf16[128,1280]{1,0:T(8,128)(2,1)S(1)}, bf16[128,1280]{1,0:T(8,128)(2,1)S(1)}, u32[]{:S(2)}, u32[]{:S(2)}) collective-permute-start(bf16[128,1280]{1,0:T(8,128)(2,1)S(1)} %get-tuple-element.60), channel_id=1, source_target_pairs={{0,2},{1,3},{2,0},{3,1},{4,6},{5,7},{6,4},{7,5},{8,10},{9,11},{10,... | collective-permute-start | bytes 983048 | tf_op jit(solution)/shard_map/ppermute | solution.py:254
  4.3 15.1 %collective-permute-start.1 = (bf16[128,1280]{1,0:T(8,128)(2,1)S(1)}, bf16[128,1280]{1,0:T(8,128)(2,1)S(1)}, u32[]{:S(2)}, u32[]{:S(2)}) collective-permute-start(bf16[128,1280]{1,0:T(8,128)(2,1)S(1)} %get-tuple-element.60), channel_id=1, source_target_pairs={{0,3},{1,0},{2,1},{3,2},{4,7},{5,4},{6,5},{7,6},{8,11},{9,8},{10,9... | collective-permute-start | bytes 983048 | tf_op jit(solution)/shard_map/ppermute | solution.py:254
  5.5 13.9 %collective-permute-start = (bf16[128,1280]{1,0:T(8,128)(2,1)S(1)}, bf16[128,1280]{1,0:T(8,128)(2,1)}, u32[]{:S(2)}, u32[]{:S(2)}) collective-permute-start(bf16[128,1280]{1,0:T(8,128)(2,1)S(1)} %get-tuple-element.60), channel_id=1, source_target_pairs={{0,1},{1,2},{2,3},{3,0},{4,5},{5,6},{6,7},{7,4},{8,9},{9,10},{10,1... | collective-permute-start | bytes 983048 | tf_op jit(solution)/shard_map/ppermute | solution.py:254
  6.3 18.4 %collective-permute-start.7 = (bf16[128,1280]{1,0:T(8,128)(2,1)S(1)}, bf16[128,1280]{1,0:T(8,128)(2,1)S(1)}, u32[]{:S(2)}, u32[]{:S(2)}) collective-permute-start(bf16[128,1280]{1,0:T(8,128)(2,1)S(1)} %get-tuple-element.59), channel_id=1, source_target_pairs={{0,64},{32,96},{64,0},{96,32},{1,65},{33,97},{65,1},{97,33},{2,66}... | collective-permute-start | bytes 983048 | tf_op jit(solution)/shard_map/ppermute | solution.py:254
  10.2 14.7 %collective-permute-start.6 = (bf16[128,1280]{1,0:T(8,128)(2,1)S(1)}, bf16[128,1280]{1,0:T(8,128)(2,1)S(1)}, u32[]{:S(2)}, u32[]{:S(2)}) collective-permute-start(bf16[128,1280]{1,0:T(8,128)(2,1)S(1)} %get-tuple-element.59), channel_id=1, source_target_pairs={{0,96},{32,0},{64,32},{96,64},{1,97},{33,1},{65,33},{97,65},{2,98}... | collective-permute-start | bytes 983048 | tf_op jit(solution)/shard_map/ppermute | solution.py:254
  13.4 12.2 %collective-permute-start.5 = (bf16[128,1280]{1,0:T(8,128)(2,1)S(1)}, bf16[128,1280]{1,0:T(8,128)(2,1)S(1)}, u32[]{:S(2)}, u32[]{:S(2)}) collective-permute-start(bf16[128,1280]{1,0:T(8,128)(2,1)S(1)} %get-tuple-element.59), channel_id=1, source_target_pairs={{0,32},{32,64},{64,96},{96,0},{1,33},{33,65},{65,97},{97,1},{2,34}... | collective-permute-start | bytes 983048 | tf_op jit(solution)/shard_map/ppermute | solution.py:254
  20.6 33.1 %collective-permute-start.3 = (bf16[128,5120]{1,0:T(8,128)(2,1)S(1)}, bf16[128,5120]{1,0:T(8,128)(2,1)}, u32[]{:S(2)}, u32[]{:S(2)}) collective-permute-start(bf16[128,5120]{1,0:T(8,128)(2,1)S(1)} %pad_maximum_fusion.refs_0_), channel_id=1, source_target_pairs={{0,32},{32,64},{64,96},{96,0},{1,33},{33,65},{65,97},{97,1},{2,34}... | collective-permute-start | bytes 3932168 | tf_op jit(solution)/shard_map/ppermute | solution.py:295
  22.5 32.7 %collective-permute-start.4 = (bf16[128,5120]{1,0:T(8,128)(2,1)S(1)}, bf16[128,5120]{1,0:T(8,128)(2,1)}, u32[]{:S(2)}, u32[]{:S(2)}) collective-permute-start(bf16[128,5120]{1,0:T(8,128)(2,1)S(1)} %pad_maximum_fusion.refs_0_), channel_id=1, source_target_pairs={{0,96},{32,0},{64,32},{96,64},{1,97},{33,1},{65,33},{97,65},{2,98}... | collective-permute-start | bytes 3932168 | tf_op jit(solution)/shard_map/ppermute | solution.py:297
  26.7 32.7 %collective-permute-start.8 = (bf16[512,1280]{1,0:T(8,128)(2,1)S(1)}, bf16[512,1280]{1,0:T(8,128)(2,1)}, u32[]{:S(2)}, u32[]{:S(2)}) collective-permute-start(bf16[512,1280]{1,0:T(8,128)(2,1)S(1)} %pad_maximum_fusion.1.refs_1_), channel_id=1, source_target_pairs={{0,1},{1,2},{2,3},{3,0},{4,5},{5,6},{6,7},{7,4},{8,9},{9,10},{10,1... | collective-permute-start | bytes 3932168 | tf_op jit(solution)/shard_map/ppermute | solution.py:296
  28.1 33.9 %collective-permute-start.9 = (bf16[512,1280]{1,0:T(8,128)(2,1)S(1)}, bf16[512,1280]{1,0:T(8,128)(2,1)}, u32[]{:S(2)}, u32[]{:S(2)}) collective-permute-start(bf16[512,1280]{1,0:T(8,128)(2,1)S(1)} %pad_maximum_fusion.1.refs_1_), channel_id=1, source_target_pairs={{0,3},{1,0},{2,1},{3,2},{4,7},{5,4},{6,5},{7,6},{8,11},{9,8},{10,9... | collective-permute-start | bytes 3932168 | tf_op jit(solution)/shard_map/ppermute | solution.py:298
  54.8 20.6 %collective-permute-start.10 = (bf16[64,5120]{1,0:T(8,128)(2,1)S(1)}, bf16[64,5120]{1,0:T(8,128)(2,1)S(1)}, u32[]{:S(2)}, u32[]{:S(2)}) collective-permute-start(bf16[64,5120]{1,0:T(8,128)(2,1)S(1)} %slice.88), channel_id=1, source_target_pairs={{0,32},{32,64},{64,96},{96,0},{1,33},{33,65},{65,97},{97,1},{2,34}... | collective-permute-start | bytes 1966088 | tf_op jit(solution)/shard_map/ppermute | solution.py:300
  56.4 20.7 %collective-permute-start.11 = (bf16[64,5120]{1,0:T(8,128)(2,1)S(1)}, bf16[64,5120]{1,0:T(8,128)(2,1)S(1)}, u32[]{:S(2)}, u32[]{:S(2)}) collective-permute-start(bf16[64,5120]{1,0:T(8,128)(2,1)S(1)} %slice.89), channel_id=1, source_target_pairs={{0,96},{32,0},{64,32},{96,64},{1,97},{33,1},{65,33},{97,65},{2,98}... | collective-permute-start | bytes 1966088 | tf_op jit(solution)/shard_map/ppermute | solution.py:301
  60.5 16.8 %collective-permute-start.12 = (bf16[256,1280]{1,0:T(8,128)(2,1)S(1)}, bf16[256,1280]{1,0:T(8,128)(2,1)S(1)}, u32[]{:S(2)}, u32[]{:S(2)}) collective-permute-start(bf16[256,1280]{1,0:T(8,128)(2,1)S(1)} %slice.90), channel_id=1, source_target_pairs={{0,1},{1,2},{2,3},{3,0},{4,5},{5,6},{6,7},{7,4},{8,9},{9,10},{10,1... | collective-permute-start | bytes 1966088 | tf_op jit(solution)/shard_map/ppermute | solution.py:302
  63.2 15.3 %collective-permute-start.13 = (bf16[256,1280]{1,0:T(8,128)(2,1)S(1)}, bf16[256,1280]{1,0:T(8,128)(2,1)S(1)}, u32[]{:S(2)}, u32[]{:S(2)}) collective-permute-start(bf16[256,1280]{1,0:T(8,128)(2,1)S(1)} %slice.91), channel_id=1, source_target_pairs={{0,3},{1,0},{2,1},{3,2},{4,7},{5,4},{6,5},{7,6},{8,11},{9,8},{10,9... | collective-permute-start | bytes 1966088 | tf_op jit(solution)/shard_map/ppermute | solution.py:303
  73.8 12.5 %collective-permute-start.15 = (bf16[768,256]{1,0:T(8,128)(2,1)S(1)}, bf16[768,256]{1,0:T(8,128)(2,1)S(1)}, u32[]{:S(2)}, u32[]{:S(2)}) collective-permute-start(bf16[768,256]{1,0:T(8,128)(2,1)S(1)} %pad_maximum_fusion.6.refs_0_), channel_id=1, source_target_pairs={{0,8},{4,12},{8,16},{12,20},{16,24},{20,28},{24,0},{28,4},{1,9},{5... | collective-permute-start | bytes 1179656 | tf_op jit(solution)/shard_map/ppermute | solution.py:310
  75.4 10.9 %collective-permute-start.16 = (bf16[768,256]{1,0:T(8,128)(2,1)S(1)}, bf16[768,256]{1,0:T(8,128)(2,1)S(1)}, u32[]{:S(2)}, u32[]{:S(2)}) collective-permute-start(bf16[768,256]{1,0:T(8,128)(2,1)S(1)} %pad_maximum_fusion.6.refs_0_), channel_id=1, source_target_pairs={{0,24},{4,28},{8,0},{12,4},{16,8},{20,12},{24,16},{28,20},{1,25},{... | collective-permute-start | bytes 1179656 | tf_op jit(solution)/shard_map/ppermute | solution.py:310
  86.3 12.7 %collective-permute-start.18 = (bf16[384,256]{1,0:T(8,128)(2,1)S(1)}, bf16[384,256]{1,0:T(8,128)(2,1)S(1)}, u32[]{:S(2)}, u32[]{:S(2)}) collective-permute-start(bf16[384,256]{1,0:T(8,128)(2,1)S(1)} %slice.73), channel_id=1, source_target_pairs={{0,8},{4,12},{8,16},{12,20},{16,24},{20,28},{24,0},{28,4},{1,9},{5... | collective-permute-start | bytes 589832 | tf_op jit(solution)/shard_map/ppermute | solution.py:314
  88.0 11.1 %collective-permute-start.19 = (bf16[384,256]{1,0:T(8,128)(2,1)S(1)}, bf16[384,256]{1,0:T(8,128)(2,1)S(1)}, u32[]{:S(2)}, u32[]{:S(2)}) collective-permute-start(bf16[384,256]{1,0:T(8,128)(2,1)S(1)} %slice.74), channel_id=1, source_target_pairs={{0,24},{4,28},{8,0},{12,4},{16,8},{20,12},{24,16},{28,20},{1,25},{... | collective-permute-start | bytes 589832 | tf_op jit(solution)/shard_map/ppermute | solution.py:314
  89.8 19.4 %collective-permute-start.20 = (bf16[1280,256]{1,0:T(8,128)(2,1)S(1)}, bf16[1280,256]{1,0:T(8,128)(2,1)S(1)}, u32[]{:S(2)}, u32[]{:S(2)}) collective-permute-start(bf16[1280,256]{1,0:T(8,128)(2,1)S(1)} %pad_maximum_fusion.2.refs_5_), channel_id=1, source_target_pairs={{0,8},{4,12},{8,16},{12,20},{16,24},{20,28},{24,0},{28,4},{1,9},{5... | collective-permute-start | bytes 1966088 | tf_op jit(solution)/shard_map/ppermute | solution.py:310
  90.2 19.2 %collective-permute-start.21 = (bf16[1280,256]{1,0:T(8,128)(2,1)S(1)}, bf16[1280,256]{1,0:T(8,128)(2,1)S(1)}, u32[]{:S(2)}, u32[]{:S(2)}) collective-permute-start(bf16[1280,256]{1,0:T(8,128)(2,1)S(1)} %pad_maximum_fusion.2.refs_5_), channel_id=1, source_target_pairs={{0,24},{4,28},{8,0},{12,4},{16,8},{20,12},{24,16},{28,20},{1,25},{... | collective-permute-start | bytes 1966088 | tf_op jit(solution)/shard_map/ppermute | solution.py:310
  109.2 11.6 %collective-permute-start.22 = (bf16[640,256]{1,0:T(8,128)(2,1)S(1)}, bf16[640,256]{1,0:T(8,128)(2,1)S(1)}, u32[]{:S(2)}, u32[]{:S(2)}) collective-permute-start(bf16[640,256]{1,0:T(8,128)(2,1)S(1)} %slice.96), channel_id=1, source_target_pairs={{0,8},{4,12},{8,16},{12,20},{16,24},{20,28},{24,0},{28,4},{1,9},{5... | collective-permute-start | bytes 983048 | tf_op jit(solution)/shard_map/ppermute | solution.py:314
  109.4 11.4 %collective-permute-start.23 = (bf16[640,256]{1,0:T(8,128)(2,1)S(1)}, bf16[640,256]{1,0:T(8,128)(2,1)S(1)}, u32[]{:S(2)}, u32[]{:S(2)}) collective-permute-start(bf16[640,256]{1,0:T(8,128)(2,1)S(1)} %slice.97), channel_id=1, source_target_pairs={{0,24},{4,28},{8,0},{12,4},{16,8},{20,12},{24,16},{28,20},{1,25},{... | collective-permute-start | bytes 983048 | tf_op jit(solution)/shard_map/ppermute | solution.py:314
  148.7 15.0 %collective-permute-start.31 = (bf16[256,1280]{1,0:T(8,128)(2,1)S(1)}, bf16[256,1280]{1,0:T(8,128)(2,1)S(1)}, u32[]{:S(2)}, u32[]{:S(2)}) collective-permute-start(bf16[256,1280]{1,0:T(8,128)(2,1)S(1)} %pad_maximum_fusion.4), channel_id=1, source_target_pairs={{0,3},{1,0},{2,1},{3,2},{4,7},{5,4},{6,5},{7,6},{8,11},{9,8},{10,9... | collective-permute-start | bytes 1966088 | tf_op jit(solution)/shard_map/ppermute | solution.py:357
  152.2 16.2 %collective-permute-start.29 = (bf16[256,1280]{1,0:T(8,128)(2,1)S(1)}, bf16[256,1280]{1,0:T(8,128)(2,1)S(1)}, u32[]{:S(2)}, u32[]{:S(2)}) collective-permute-start(bf16[256,1280]{1,0:T(8,128)(2,1)S(1)} %pad_maximum_fusion.3), channel_id=1, source_target_pairs={{0,1},{1,2},{2,3},{3,0},{4,5},{5,6},{6,7},{7,4},{8,9},{9,10},{10,1... | collective-permute-start | bytes 1966088 | tf_op jit(solution)/shard_map/ppermute | solution.py:356
  (17 other events, 139.5 us)

commit v2 on v1

--- a/solution.py
+++ b/solution.py
@@ -104,8 +104,33 @@
     if n_done:
         rows = jnp.concatenate([done_refs[0][...], rows], axis=0)
     emit_heads(rows, scale_ref, where_ref[4], *outs[:3])
-    if not emit_all:
+    if not emit_all and b_slices:
         outs[3][...] = acc_ref[na:]
+
+
+def part_kernel(b_slices, where_ref, w_ref, part_ref, *refs):
+    b_refs, o_ref = refs[:-1], refs[-1]
+    feat = w_ref.shape[1] // 4
+    for c in range(3):
+        cols = slice(c * 256, (c + 1) * 256)
+        d = part_ref[:, cols]
+        for i, b_ref in zip(b_slices, b_refs):
+            at = pl.ds(pl.multiple_of(where_ref[i] * feat, feat), feat)
+            d = d + jnp.dot(b_ref[...], w_ref[c, at, :], preferred_element_type=jnp.float32)
+        o_ref[:, cols] = d
+
+
+def project_part(where, w, b_parts, b_slices, part):
+    return pl.pallas_call(
+        functools.partial(part_kernel, b_slices),
+        in_specs=FIXED[:2] + [VM] * (1 + len(b_parts)),
+        out_specs=VM,
+        out_shape=jax.ShapeDtypeStruct(part.shape, part.dtype),
+        compiler_params=pltpu.CompilerParams(vmem_limit_bytes=16 << 20),
+        cost_estimate=pl.CostEstimate(
+            flops=2 * 768 * sum(x.size for x in b_parts), bytes_accessed=w.size, transcendentals=0
+        ),
+    )(where, w, part, *b_parts)
 
 
 VM = pl.BlockSpec(memory_space=pltpu.VMEM)
@@ -115,12 +140,12 @@
 def project_stage(where, w, scale, a_parts, b_parts, b_slices, done, part, emit_all):
     feat = w.shape[1] // 4
     na = sum(x.shape[0] for x in a_parts)
-    nb = 512 if part is None else part.shape[0]
+    nb = part.shape[0] if part is not None else b_parts[0].shape[0] if b_parts else 0
     f32 = lambda n: jax.ShapeDtypeStruct((n, 768), jnp.float32)
     if emit_all:
         shapes = heads_shape(na + nb)
     elif done is not None:
-        shapes = heads_shape(done.shape[0] + na) + [f32(nb)]
+        shapes = heads_shape(done.shape[0] + na) + ([f32(nb)] if b_parts else [])
     else:
         shapes = [f32(na), f32(nb)]
     extra = [x for x in (done, part) if x is not None]
@@ -297,6 +322,8 @@
     a_p = pp(a_own, "ulysses", ring(nu, -1))
     b_p = pp(b_own, "tensor", ring(nt, -1))
     ah, bh = a_own.shape[0] // 2, b_own.shape[0] // 2
+    done, part = project_stage(where, w, scale, [a_own], [b_own], (0,), None, None, False)
+    done, bias, a_m = hold((done, bias, a_m))
     a0 = pp(a_m[:ah], "ulysses", ring(nu, 1))
     a1 = pp(a_p[ah:], "ulysses", ring(nu, -1))
     b0 = pp(b_m[:bh], "tensor", ring(nt, 1))
@@ -313,12 +340,10 @@
         h = kv_m.shape[0] // 2
         return [pp(kv_m[:h], "blk", y_ring(nb, 1)), pp(kv_p[h:], "blk", y_ring(nb, -1))]
 
-    done, part = project_stage(where, w, scale, [a_own], [b_own], (0,), None, None, False)
-    done, bias = hold((done, bias))
-    q1, kv1, give1, part = project_stage(
-        where, w, scale, [a_m, a_p], [b_m, b_p], (1, 2), done, part, False
-    )
+    q1, kv1, give1 = project_stage(where, w, scale, [a_m, a_p], [], (), done, None, False)
     q1x, kv1 = swap(kv1, give1)
+    part, kv1 = hold((part, kv1))
+    part = project_part(where, w, [b_m, b_p], (1, 2), part)
     kv1_near = near_y(kv1)
     q2, kv2, give2 = project_stage(where, w, scale, [a0, a1], [b0, b1], (3, 3), None, part, True)
     give2, kv1_near = hold((give2, kv1_near))

time: 170 us -> 167 us (0.982)
  waiting for transfers between devices: 56.7 us -> 51.8 us
    pallas_call x0 -> x1, Pallas kernels: none -> 3.93 us  [project_part(): pl.pallas_call(functools.partial(part_kernel, b_slices), in_specs=FIXED[:...]
    ppermute x4, waiting for transfers between devices: 8.68 us -> 4.85 us  [near_y(): return [pp(kv, 'blk', y_ring(nb, s)) for s in (1, -1)]]
    pallas_call x3, Pallas kernels: 12.7 us -> 9.74 us  [project_stage(): pl.pallas_call(functools.partial(stage_kernel, len(a_parts), b_slices, in...]
  transfers between devices with their start and end apart: 32 -> 32, of which waited for: 15 -> 13; matrix products, arithmetic and copies ran while one was open for 5% -> 5% of each run, Pallas kernels for 24% -> 25%
where the time goes in v2:
time: 167 us
  waiting for transfers between devices  51.8 us (31%)
  starting transfers between devices  49 us (29%)
  Pallas kernels  47.7 us (29%)
  local copies, waits for them, and re-layouts  11.1 us (7%)
  other arithmetic  3.77 us (2%)
  between operations  3.02 us (2%)
    pallas_call x4, Pallas kernels, attention(): pl.pallas_call(functools.partial(attn_kernel, sizes, first_block, begin,...  24.5 us
    ppermute x1, waiting for transfers between devices, local(): a_m = pp(a_own, 'ulysses', ring(nu, 1))  13.5 us
    ppermute x6, starting transfers between devices, direct(): return [value] + [pp(value, axis, ring(n, s)) for s in (1, -1, 2)]  11.8 us
    pallas_call x3, Pallas kernels, project_stage(): pl.pallas_call(functools.partial(stage_kernel, len(a_parts), b_slices, in...  9.74 us
    ppermute x1, waiting for transfers between devices, local(): from_p = pp(to_m, 'tensor', ring(nt, -1))  9.36 us
    ppermute x4, starting transfers between devices, near_y(): return [pp(kv, 'blk', y_ring(nb, s)) for s in (1, -1)]  7.77 us
    ppermute x6, waiting for transfers between devices, direct(): return [value] + [pp(value, axis, ring(n, s)) for s in (1, -1, 2)]  6.62 us
    ppermute x2, starting transfers between devices, far_y(): pp(kv_p[h:], 'blk', y_ring(nb, -1))  5.14 us
  transfers between devices with their start and end apart: 32, of which 13 were waited for; matrix products, arithmetic and copies ran while one was open for 5% of the time, Pallas kernels for 25%

profile of v2, /device:TPU:0, one launch (start us, length us, event | category | flops | bytes accessed | tf_op | source)
XLA Modules:
  0.0 166.6 jit_solution(200574004472364537)
XLA Ops:
  1.1 3.2 %collective-permute-start.2 = (bf16[128,1280]{1,0:T(8,128)(2,1)S(1)}, bf16[128,1280]{1,0:T(8,128)(2,1)S(1)}, u32[]{:S(2)}, u32[]{:S(2)}) collective-permute-start(bf16[128,1280]{1,0:T(8,128)(2,1)S(1)} %get-tuple-element.64), channel_id=1, source_target_pairs={{0,2},{1,3},{2,0},{3,1},{4,6},{5,7},{6,4},{7,5},{8,10},{9,11},{10,... | collective-permute-start | bytes 983048 | tf_op jit(solution)/shard_map/ppermute | solution.py:279
  6.3 3.9 %collective-permute-start.5 = (bf16[128,1280]{1,0:T(8,128)(2,1)S(1)}, bf16[128,1280]{1,0:T(8,128)(2,1)S(1)}, u32[]{:S(2)}, u32[]{:S(2)}) collective-permute-start(bf16[128,1280]{1,0:T(8,128)(2,1)S(1)} %get-tuple-element.63), channel_id=1, source_target_pairs={{0,64},{32,96},{64,0},{96,32},{1,65},{33,97},{65,1},{97,33},{2,66}... | collective-permute-start | bytes 983048 | tf_op jit(solution)/shard_map/ppermute | solution.py:279
  11.0 2.4 %collective-permute-done.2 = bf16[128,1280]{1,0:T(8,128)(2,1)S(1)} collective-permute-done((bf16[128,1280]{1,0:T(8,128)(2,1)S(1)}, bf16[128,1280]{1,0:T(8,128)(2,1)S(1)}, u32[]{:S(2)}, u32[]{:S(2)}) %collective-permute-start.2) | collective-permute-done | bytes 327712 | tf_op jit(solution)/shard_map/ppermute | solution.py:279
  15.4 4.0 %collective-permute-done.1 = bf16[128,1280]{1,0:T(8,128)(2,1)S(1)} collective-permute-done((bf16[128,1280]{1,0:T(8,128)(2,1)S(1)}, bf16[128,1280]{1,0:T(8,128)(2,1)S(1)}, u32[]{:S(2)}, u32[]{:S(2)}) %collective-permute-start.1) | collective-permute-done | bytes 327712 | tf_op jit(solution)/shard_map/ppermute | solution.py:279
  34.1 3.2 %copy-done = bf16[5120,3,256]{2,0,1:T(8,128)(2,1)S(1)} copy-done((bf16[5120,3,256]{2,0,1:T(8,128)(2,1)S(1)}, bf16[5120,3,256]{2,0,1:T(8,128)(2,1)}, u32[]{:S(2)}) %copy-start) | copy-done | bytes 7864344
  37.3 2.8 %shard_map.73 = (f32[128,768]{1,0:T(8,128)S(1)}, f32[512,768]{1,0:T(8,128)S(1)}) custom-call(s32[9]{0:T(128)S(1)} %pad_add_fusion.where_ref, bf16[3,5120,256]{2,1,0:T(8,128)(2,1)S(1)} %bitcast.87, f32[1,768]{1,0:T(1,128)S(1)} %bitcast.99, bf16[128,5120]{1,0:T(8,128)(2,1)S(1)} %pad_maximum_fusion.refs_0_, bf16[512,1280]{1,0:T(8,128)(2,1)S(1)} %pad_maximum_fusion.1.refs_1_), custom_call_target="tpu_custom_call" | custom-call | flops 2013265920 | bytes 7864320 | tf_op jit(solution)/shard_map/pallas_call | solution.py:152
  40.2 13.5 %collective-permute-done.6.refs_0_ = bf16[128,5120]{1,0:T(8,128)(2,1)} collective-permute-done((bf16[128,5120]{1,0:T(8,128)(2,1)S(1)}, bf16[128,5120]{1,0:T(8,128)(2,1)}, u32[]{:S(2)}, u32[]{:S(2)}) %collective-permute-start.6) | collective-permute-done | bytes 1310752 | tf_op jit(solution)/shard_map/ppermute | solution.py:320
  56.5 3.0 %collective-permute-start.9 = (bf16[64,5120]{1,0:T(8,128)(2,1)S(1)}, bf16[64,5120]{1,0:T(8,128)(2,1)S(1)}, u32[]{:S(2)}, u32[]{:S(2)}) collective-permute-start(bf16[64,5120]{1,0:T(8,128)(2,1)S(1)} %slice.88), channel_id=1, source_target_pairs={{0,96},{32,0},{64,32},{96,64},{1,97},{33,1},{65,33},{97,65},{2,98}... | collective-permute-start | bytes 1966088 | tf_op jit(solution)/shard_map/ppermute | solution.py:328
  65.1 4.0 %shard_map.74 = (bf16[384,128]{1,0:T(8,128)(2,1)S(1)}, bf16[384,256]{1,0:T(8,128)(2,1)S(1)}, bf16[384,384]{1,0:T(8,128)(2,1)S(1)}) custom-call(s32[9]{0:T(128)S(1)} %pad_add_fusion.where_ref, bf16[3,5120,256]{2,1,0:T(8,128)(2,1)S(1)} %bitcast.88, f32[1,768]{1,0:T(1,128)S(1)} %bitcast.100, bf16[128,5120]{1,0:T(8,128)(2,1)} %collective-permute-done.6.refs_0_, ...), custom_call_target="tpu_custom_call" | custom-call | flops 2013265920 | bytes 7864320 | tf_op jit(solution)/shard_map/pallas_call | solution.py:152
  72.5 2.8 %collective-permute-start.16 = (bf16[768,256]{1,0:T(8,128)(2,1)S(1)}, bf16[768,256]{1,0:T(8,128)(2,1)S(1)}, u32[]{:S(2)}, u32[]{:S(2)}) collective-permute-start(bf16[768,256]{1,0:T(8,128)(2,1)S(1)} %pad_maximum_fusion.6.refs_0_), channel_id=1, source_target_pairs={{0,24},{4,28},{8,0},{12,4},{16,8},{20,12},{24,16},{28,20},{1,25},{... | collective-permute-start | bytes 1179656 | tf_op jit(solution)/shard_map/ppermute | solution.py:337
  75.3 3.9 %shard_map.75.refs_4_ = f32[512,768]{1,0:T(8,128)S(1)} custom-call(s32[9]{0:T(128)S(1)} %pad_add_fusion.where_ref, bf16[3,5120,256]{2,1,0:T(8,128)(2,1)S(1)} %bitcast.89, f32[512,768]{1,0:T(8,128)S(1)} %get-tuple-element.41.part_ref, bf16[512,1280]{1,0:T(8,128)(2,1)} %collective-permute-done.10.refs_0_, bf16[512,1280]{1,0:T(8,128)(2,1)} %collective-permute-done.12.refs_1_), custom_call_target="tpu_custom_call" | custom-call | flops 2013265920 | bytes 3932160 | tf_op jit(solution)/shard_map/pallas_call | solution.py:124
  79.3 2.9 %shard_map.76 = (bf16[640,128]{1,0:T(8,128)(2,1)S(1)}, bf16[640,256]{1,0:T(8,128)(2,1)S(1)}, bf16[640,384]{1,0:T(8,128)(2,1)S(1)}) custom-call(s32[9]{0:T(128)S(1)} %pad_add_fusion.where_ref, bf16[3,5120,256]{2,1,0:T(8,128)(2,1)S(1)} %bitcast.90, f32[1,768]{1,0:T(1,128)S(1)} %bitcast.101, bf16[64,5120]{1,0:T(8,128)(2,1)S(1)} %collective-permute-done.8.refs_0_, ...), custom_call_target="tpu_custom_call" | custom-call | flops 2013265920 | bytes 7864320 | tf_op jit(solution)/shard_map/pallas_call | solution.py:152
  87.3 2.9 %collective-permute-start.21 = (bf16[1280,256]{1,0:T(8,128)(2,1)S(1)}, bf16[1280,256]{1,0:T(8,128)(2,1)S(1)}, u32[]{:S(2)}, u32[]{:S(2)}) collective-permute-start(bf16[1280,256]{1,0:T(8,128)(2,1)S(1)} %pad_maximum_fusion.2.refs_5_), channel_id=1, source_target_pairs={{0,24},{4,28},{8,0},{12,4},{16,8},{20,12},{24,16},{28,20},{1,25},{... | collective-permute-start | bytes 1966088 | tf_op jit(solution)/shard_map/ppermute | solution.py:337
  90.2 6.0 %shard_map.77 = (f32[2048,128]{1,0:T(8,128)S(1)}, f32[2048,128]{1,0:T(8,128)S(1)}, f32[2048,128]{1,0:T(8,128)S(1)}) custom-call(bf16[2048,128]{1,0:T(8,128)(2,1)S(1)} %pad_maximum_fusion.5.q_ref, bf16[2048,128]{1,0:T(8,128)(2,1)S(1)} %bitcast.95, bf16[768,256]{1,0:T(8,128)(2,1)S(1)} %pad_maximum_fusion.6.refs_0_, ...), custom_call_target="tpu_custom_call" | custom-call | flops 4831838208 | bytes 1179648 | tf_op jit(solution)/shard_map/pallas_call | solution.py:255
  96.2 6.3 %shard_map.78 = (f32[2048,128]{1,0:T(8,128)S(1)}, f32[2048,128]{1,0:T(8,128)S(1)}, f32[2048,128]{1,0:T(8,128)S(1)}) custom-call(bf16[2048,128]{1,0:T(8,128)(2,1)S(1)} %pad_maximum_fusion.5.q_ref, bf16[2048,128]{1,0:T(8,128)(2,1)S(1)} %bitcast.96, f32[2048,128]{1,0:T(8,128)S(1)} %get-tuple-element.49.refs_0_, f32[2048,128]{1,0:T(8,128)S(1)} %get-tuple-element.50.refs_1_, ...), custom_call_target="tpu_custom_call" | custom-call | flops 4294967296 | bytes 1048576 | tf_op jit(solution)/shard_map/pallas_call | solution.py:255
  102.6 3.7 %collective-permute-done.20.refs_3_ = bf16[1280,256]{1,0:T(8,128)(2,1)S(1)} collective-permute-done((bf16[1280,256]{1,0:T(8,128)(2,1)S(1)}, bf16[1280,256]{1,0:T(8,128)(2,1)S(1)}, u32[]{:S(2)}, u32[]{:S(2)}) %collective-permute-start.20) | collective-permute-done | bytes 655392 | tf_op jit(solution)/shard_map/ppermute | solution.py:337
  106.5 3.4 %collective-permute-start.23 = (bf16[640,256]{1,0:T(8,128)(2,1)S(1)}, bf16[640,256]{1,0:T(8,128)(2,1)S(1)}, u32[]{:S(2)}, u32[]{:S(2)}) collective-permute-start(bf16[640,256]{1,0:T(8,128)(2,1)S(1)} %slice.96), channel_id=1, source_target_pairs={{0,24},{4,28},{8,0},{12,4},{16,8},{20,12},{24,16},{28,20},{1,25},{... | collective-permute-start | bytes 983048 | tf_op jit(solution)/shard_map/ppermute | solution.py:341
  109.9 7.9 %shard_map.79 = (f32[2048,128]{1,0:T(8,128)S(1)}, f32[2048,128]{1,0:T(8,128)S(1)}, f32[2048,128]{1,0:T(8,128)S(1)}) custom-call(bf16[2048,128]{1,0:T(8,128)(2,1)S(1)} %pad_maximum_fusion.5.q_ref, bf16[2048,128]{1,0:T(8,128)(2,1)S(1)} %bitcast.97, f32[2048,128]{1,0:T(8,128)S(1)} %get-tuple-element.53.refs_0_, f32[2048,128]{1,0:T(8,128)S(1)} %get-tuple-element.54.refs_1_, ...), custom_call_target="tpu_custom_call" | custom-call | flops 5368709120 | bytes 1310720 | tf_op jit(solution)/shard_map/pallas_call | solution.py:255
  117.9 4.3 %shard_map.80 = bf16[2048,128]{1,0:T(8,128)(2,1)S(1)} custom-call(bf16[2048,128]{1,0:T(8,128)(2,1)S(1)} %pad_maximum_fusion.5.q_ref, bf16[2048,128]{1,0:T(8,128)(2,1)S(1)} %bitcast.98, f32[2048,128]{1,0:T(8,128)S(1)} %get-tuple-element.56.refs_0_, f32[2048,128]{1,0:T(8,128)S(1)} %get-tuple-element.57.refs_1_, f32[2048,128]{1,0:T(8,128)S(1)} %get-tuple-element.58.refs_2_, ...), custom_call_target="tpu_custom_call" | custom-call | flops 2684354560 | bytes 655360 | tf_op jit(solution)/shard_map/pallas_call | solution.py:255
  127.5 4.7 %shard_map.81.refs_4_ = bf16[4,4,256,1280]{3,2,1,0:T(8,128)(2,1)S(1)} custom-call(s32[9]{0:T(128)S(1)} %pad_add_fusion.where_ref, bf16[256,256]{1,0:T(8,128)(2,1)S(1)} %bitcast.91, bf16[4,256,5120]{2,1,0:T(8,128)(2,1)} %hbm.1), custom_call_target="tpu_custom_call" | custom-call | bytes 20971520 | tf_op jit(solution)/shard_map/pallas_call | solution.py:65
  132.2 3.0 %collective-permute-done.26.refs_2_ = bf16[256,256]{1,0:T(8,128)(2,1)S(1)} collective-permute-done((bf16[256,256]{1,0:T(8,128)(2,1)S(1)}, bf16[256,256]{1,0:T(8,128)(2,1)S(1)}, u32[]{:S(2)}, u32[]{:S(2)}) %collective-permute-start.26) | collective-permute-done | bytes 131104 | tf_op jit(solution)/shard_map/ppermute | solution.py:369
  141.0 4.6 %collective-permute-done.30 = bf16[128,1280]{1,0:T(8,128)(2,1)S(1)} collective-permute-done((bf16[128,1280]{1,0:T(8,128)(2,1)S(1)}, bf16[128,1280]{1,0:T(8,128)(2,1)S(1)}, u32[]{:S(2)}, u32[]{:S(2)}) %collective-permute-start.30) | collective-permute-done | bytes 327712 | tf_op jit(solution)/shard_map/ppermute | solution.py:377
  151.3 9.4 %collective-permute-done.31 = bf16[256,1280]{1,0:T(8,128)(2,1)S(1)} collective-permute-done((bf16[256,1280]{1,0:T(8,128)(2,1)S(1)}, bf16[256,1280]{1,0:T(8,128)(2,1)S(1)}, u32[]{:S(2)}, u32[]{:S(2)}) %collective-permute-start.31) | collective-permute-done | bytes 655392 | tf_op jit(solution)/shard_map/ppermute | solution.py:382
  160.7 4.9 %collective-permute-done.29 = bf16[256,1280]{1,0:T(8,128)(2,1)S(1)} collective-permute-done((bf16[256,1280]{1,0:T(8,128)(2,1)S(1)}, bf16[256,1280]{1,0:T(8,128)(2,1)S(1)}, u32[]{:S(2)}, u32[]{:S(2)}) %collective-permute-start.29) | collective-permute-done | bytes 655392 | tf_op jit(solution)/shard_map/ppermute | solution.py:381
  (112 shorter events, 52.9 us)
Async XLA Ops:
  1.1 12.2 %collective-permute-start.2 = (bf16[128,1280]{1,0:T(8,128)(2,1)S(1)}, bf16[128,1280]{1,0:T(8,128)(2,1)S(1)}, u32[]{:S(2)}, u32[]{:S(2)}) collective-permute-start(bf16[128,1280]{1,0:T(8,128)(2,1)S(1)} %get-tuple-element.64), channel_id=1, source_target_pairs={{0,2},{1,3},{2,0},{3,1},{4,6},{5,7},{6,4},{7,5},{8,10},{9,11},{10,... | collective-permute-start | bytes 983048 | tf_op jit(solution)/shard_map/ppermute | solution.py:279
  4.3 15.1 %collective-permute-start.1 = (bf16[128,1280]{1,0:T(8,128)(2,1)S(1)}, bf16[128,1280]{1,0:T(8,128)(2,1)S(1)}, u32[]{:S(2)}, u32[]{:S(2)}) collective-permute-start(bf16[128,1280]{1,0:T(8,128)(2,1)S(1)} %get-tuple-element.64), channel_id=1, source_target_pairs={{0,3},{1,0},{2,1},{3,2},{4,7},{5,4},{6,5},{7,6},{8,11},{9,8},{10,9... | collective-permute-start | bytes 983048 | tf_op jit(solution)/shard_map/ppermute | solution.py:279
  5.5 13.9 %collective-permute-start = (bf16[128,1280]{1,0:T(8,128)(2,1)S(1)}, bf16[128,1280]{1,0:T(8,128)(2,1)}, u32[]{:S(2)}, u32[]{:S(2)}) collective-permute-start(bf16[128,1280]{1,0:T(8,128)(2,1)S(1)} %get-tuple-element.64), channel_id=1, source_target_pairs={{0,1},{1,2},{2,3},{3,0},{4,5},{5,6},{6,7},{7,4},{8,9},{9,10},{10,1... | collective-permute-start | bytes 983048 | tf_op jit(solution)/shard_map/ppermute | solution.py:279
  6.3 18.4 %collective-permute-start.5 = (bf16[128,1280]{1,0:T(8,128)(2,1)S(1)}, bf16[128,1280]{1,0:T(8,128)(2,1)S(1)}, u32[]{:S(2)}, u32[]{:S(2)}) collective-permute-start(bf16[128,1280]{1,0:T(8,128)(2,1)S(1)} %get-tuple-element.63), channel_id=1, source_target_pairs={{0,64},{32,96},{64,0},{96,32},{1,65},{33,97},{65,1},{97,33},{2,66}... | collective-permute-start | bytes 983048 | tf_op jit(solution)/shard_map/ppermute | solution.py:279
  10.2 14.7 %collective-permute-start.4 = (bf16[128,1280]{1,0:T(8,128)(2,1)S(1)}, bf16[128,1280]{1,0:T(8,128)(2,1)S(1)}, u32[]{:S(2)}, u32[]{:S(2)}) collective-permute-start(bf16[128,1280]{1,0:T(8,128)(2,1)S(1)} %get-tuple-element.63), channel_id=1, source_target_pairs={{0,96},{32,0},{64,32},{96,64},{1,97},{33,1},{65,33},{97,65},{2,98}... | collective-permute-start | bytes 983048 | tf_op jit(solution)/shard_map/ppermute | solution.py:279
  13.4 12.2 %collective-permute-start.3 = (bf16[128,1280]{1,0:T(8,128)(2,1)S(1)}, bf16[128,1280]{1,0:T(8,128)(2,1)S(1)}, u32[]{:S(2)}, u32[]{:S(2)}) collective-permute-start(bf16[128,1280]{1,0:T(8,128)(2,1)S(1)} %get-tuple-element.63), channel_id=1, source_target_pairs={{0,32},{32,64},{64,96},{96,0},{1,33},{33,65},{65,97},{97,1},{2,34}... | collective-permute-start | bytes 983048 | tf_op jit(solution)/shard_map/ppermute | solution.py:279
  20.6 33.1 %collective-permute-start.6 = (bf16[128,5120]{1,0:T(8,128)(2,1)S(1)}, bf16[128,5120]{1,0:T(8,128)(2,1)}, u32[]{:S(2)}, u32[]{:S(2)}) collective-permute-start(bf16[128,5120]{1,0:T(8,128)(2,1)S(1)} %pad_maximum_fusion.refs_0_), channel_id=1, source_target_pairs={{0,32},{32,64},{64,96},{96,0},{1,33},{33,65},{65,97},{97,1},{2,34}... | collective-permute-start | bytes 3932168 | tf_op jit(solution)/shard_map/ppermute | solution.py:320
  22.5 32.8 %collective-permute-start.7 = (bf16[128,5120]{1,0:T(8,128)(2,1)S(1)}, bf16[128,5120]{1,0:T(8,128)(2,1)}, u32[]{:S(2)}, u32[]{:S(2)}) collective-permute-start(bf16[128,5120]{1,0:T(8,128)(2,1)S(1)} %pad_maximum_fusion.refs_0_), channel_id=1, source_target_pairs={{0,96},{32,0},{64,32},{96,64},{1,97},{33,1},{65,33},{97,65},{2,98}... | collective-permute-start | bytes 3932168 | tf_op jit(solution)/shard_map/ppermute | solution.py:322
  26.7 32.7 %collective-permute-start.10 = (bf16[512,1280]{1,0:T(8,128)(2,1)S(1)}, bf16[512,1280]{1,0:T(8,128)(2,1)}, u32[]{:S(2)}, u32[]{:S(2)}) collective-permute-start(bf16[512,1280]{1,0:T(8,128)(2,1)S(1)} %pad_maximum_fusion.1.refs_1_), channel_id=1, source_target_pairs={{0,1},{1,2},{2,3},{3,0},{4,5},{5,6},{6,7},{7,4},{8,9},{9,10},{10,1... | collective-permute-start | bytes 3932168 | tf_op jit(solution)/shard_map/ppermute | solution.py:321
  28.1 34.0 %collective-permute-start.12 = (bf16[512,1280]{1,0:T(8,128)(2,1)S(1)}, bf16[512,1280]{1,0:T(8,128)(2,1)}, u32[]{:S(2)}, u32[]{:S(2)}) collective-permute-start(bf16[512,1280]{1,0:T(8,128)(2,1)S(1)} %pad_maximum_fusion.1.refs_1_), channel_id=1, source_target_pairs={{0,3},{1,0},{2,1},{3,2},{4,7},{5,4},{6,5},{7,6},{8,11},{9,8},{10,9... | collective-permute-start | bytes 3932168 | tf_op jit(solution)/shard_map/ppermute | solution.py:323
  54.9 17.6 %collective-permute-start.8 = (bf16[64,5120]{1,0:T(8,128)(2,1)S(1)}, bf16[64,5120]{1,0:T(8,128)(2,1)S(1)}, u32[]{:S(2)}, u32[]{:S(2)}) collective-permute-start(bf16[64,5120]{1,0:T(8,128)(2,1)S(1)} %slice.66), channel_id=1, source_target_pairs={{0,32},{32,64},{64,96},{96,0},{1,33},{33,65},{65,97},{97,1},{2,34}... | collective-permute-start | bytes 1966088 | tf_op jit(solution)/shard_map/ppermute | solution.py:327
  56.5 22.8 %collective-permute-start.9 = (bf16[64,5120]{1,0:T(8,128)(2,1)S(1)}, bf16[64,5120]{1,0:T(8,128)(2,1)S(1)}, u32[]{:S(2)}, u32[]{:S(2)}) collective-permute-start(bf16[64,5120]{1,0:T(8,128)(2,1)S(1)} %slice.88), channel_id=1, source_target_pairs={{0,96},{32,0},{64,32},{96,64},{1,97},{33,1},{65,33},{97,65},{2,98}... | collective-permute-start | bytes 1966088 | tf_op jit(solution)/shard_map/ppermute | solution.py:328
  60.6 18.7 %collective-permute-start.11 = (bf16[256,1280]{1,0:T(8,128)(2,1)S(1)}, bf16[256,1280]{1,0:T(8,128)(2,1)S(1)}, u32[]{:S(2)}, u32[]{:S(2)}) collective-permute-start(bf16[256,1280]{1,0:T(8,128)(2,1)S(1)} %slice.89), channel_id=1, source_target_pairs={{0,1},{1,2},{2,3},{3,0},{4,5},{5,6},{6,7},{7,4},{8,9},{9,10},{10,1... | collective-permute-start | bytes 1966088 | tf_op jit(solution)/shard_map/ppermute | solution.py:329
  63.3 16.0 %collective-permute-start.13 = (bf16[256,1280]{1,0:T(8,128)(2,1)S(1)}, bf16[256,1280]{1,0:T(8,128)(2,1)S(1)}, u32[]{:S(2)}, u32[]{:S(2)}) collective-permute-start(bf16[256,1280]{1,0:T(8,128)(2,1)S(1)} %slice.90), channel_id=1, source_target_pairs={{0,3},{1,0},{2,1},{3,2},{4,7},{5,4},{6,5},{7,6},{8,11},{9,8},{10,9... | collective-permute-start | bytes 1966088 | tf_op jit(solution)/shard_map/ppermute | solution.py:330
  70.8 12.5 %collective-permute-start.15 = (bf16[768,256]{1,0:T(8,128)(2,1)S(1)}, bf16[768,256]{1,0:T(8,128)(2,1)S(1)}, u32[]{:S(2)}, u32[]{:S(2)}) collective-permute-start(bf16[768,256]{1,0:T(8,128)(2,1)S(1)} %pad_maximum_fusion.6.refs_0_), channel_id=1, source_target_pairs={{0,8},{4,12},{8,16},{12,20},{16,24},{20,28},{24,0},{28,4},{1,9},{5... | collective-permute-start | bytes 1179656 | tf_op jit(solution)/shard_map/ppermute | solution.py:337
  72.5 10.9 %collective-permute-start.16 = (bf16[768,256]{1,0:T(8,128)(2,1)S(1)}, bf16[768,256]{1,0:T(8,128)(2,1)S(1)}, u32[]{:S(2)}, u32[]{:S(2)}) collective-permute-start(bf16[768,256]{1,0:T(8,128)(2,1)S(1)} %pad_maximum_fusion.6.refs_0_), channel_id=1, source_target_pairs={{0,24},{4,28},{8,0},{12,4},{16,8},{20,12},{24,16},{28,20},{1,25},{... | collective-permute-start | bytes 1179656 | tf_op jit(solution)/shard_map/ppermute | solution.py:337
  83.4 12.8 %collective-permute-start.18 = (bf16[384,256]{1,0:T(8,128)(2,1)S(1)}, bf16[384,256]{1,0:T(8,128)(2,1)S(1)}, u32[]{:S(2)}, u32[]{:S(2)}) collective-permute-start(bf16[384,256]{1,0:T(8,128)(2,1)S(1)} %slice.73), channel_id=1, source_target_pairs={{0,8},{4,12},{8,16},{12,20},{16,24},{20,28},{24,0},{28,4},{1,9},{5... | collective-permute-start | bytes 589832 | tf_op jit(solution)/shard_map/ppermute | solution.py:341
  85.0 11.2 %collective-permute-start.19 = (bf16[384,256]{1,0:T(8,128)(2,1)S(1)}, bf16[384,256]{1,0:T(8,128)(2,1)S(1)}, u32[]{:S(2)}, u32[]{:S(2)}) collective-permute-start(bf16[384,256]{1,0:T(8,128)(2,1)S(1)} %slice.74), channel_id=1, source_target_pairs={{0,24},{4,28},{8,0},{12,4},{16,8},{20,12},{24,16},{28,20},{1,25},{... | collective-permute-start | bytes 589832 | tf_op jit(solution)/shard_map/ppermute | solution.py:341
  86.9 19.4 %collective-permute-start.20 = (bf16[1280,256]{1,0:T(8,128)(2,1)S(1)}, bf16[1280,256]{1,0:T(8,128)(2,1)S(1)}, u32[]{:S(2)}, u32[]{:S(2)}) collective-permute-start(bf16[1280,256]{1,0:T(8,128)(2,1)S(1)} %pad_maximum_fusion.2.refs_5_), channel_id=1, source_target_pairs={{0,8},{4,12},{8,16},{12,20},{16,24},{20,28},{24,0},{28,4},{1,9},{5... | collective-permute-start | bytes 1966088 | tf_op jit(solution)/shard_map/ppermute | solution.py:337
  87.3 19.2 %collective-permute-start.21 = (bf16[1280,256]{1,0:T(8,128)(2,1)S(1)}, bf16[1280,256]{1,0:T(8,128)(2,1)S(1)}, u32[]{:S(2)}, u32[]{:S(2)}) collective-permute-start(bf16[1280,256]{1,0:T(8,128)(2,1)S(1)} %pad_maximum_fusion.2.refs_5_), channel_id=1, source_target_pairs={{0,24},{4,28},{8,0},{12,4},{16,8},{20,12},{24,16},{28,20},{1,25},{... | collective-permute-start | bytes 1966088 | tf_op jit(solution)/shard_map/ppermute | solution.py:337
  106.3 11.6 %collective-permute-start.22 = (bf16[640,256]{1,0:T(8,128)(2,1)S(1)}, bf16[640,256]{1,0:T(8,128)(2,1)S(1)}, u32[]{:S(2)}, u32[]{:S(2)}) collective-permute-start(bf16[640,256]{1,0:T(8,128)(2,1)S(1)} %slice.95), channel_id=1, source_target_pairs={{0,8},{4,12},{8,16},{12,20},{16,24},{20,28},{24,0},{28,4},{1,9},{5... | collective-permute-start | bytes 983048 | tf_op jit(solution)/shard_map/ppermute | solution.py:341
  106.5 11.4 %collective-permute-start.23 = (bf16[640,256]{1,0:T(8,128)(2,1)S(1)}, bf16[640,256]{1,0:T(8,128)(2,1)S(1)}, u32[]{:S(2)}, u32[]{:S(2)}) collective-permute-start(bf16[640,256]{1,0:T(8,128)(2,1)S(1)} %slice.96), channel_id=1, source_target_pairs={{0,24},{4,28},{8,0},{12,4},{16,8},{20,12},{24,16},{28,20},{1,25},{... | collective-permute-start | bytes 983048 | tf_op jit(solution)/shard_map/ppermute | solution.py:341
  145.7 15.0 %collective-permute-start.31 = (bf16[256,1280]{1,0:T(8,128)(2,1)S(1)}, bf16[256,1280]{1,0:T(8,128)(2,1)S(1)}, u32[]{:S(2)}, u32[]{:S(2)}) collective-permute-start(bf16[256,1280]{1,0:T(8,128)(2,1)S(1)} %pad_maximum_fusion.4), channel_id=1, source_target_pairs={{0,3},{1,0},{2,1},{3,2},{4,7},{5,4},{6,5},{7,6},{8,11},{9,8},{10,9... | collective-permute-start | bytes 1966088 | tf_op jit(solution)/shard_map/ppermute | solution.py:382
  149.9 15.7 %collective-permute-start.29 = (bf16[256,1280]{1,0:T(8,128)(2,1)S(1)}, bf16[256,1280]{1,0:T(8,128)(2,1)S(1)}, u32[]{:S(2)}, u32[]{:S(2)}) collective-permute-start(bf16[256,1280]{1,0:T(8,128)(2,1)S(1)} %pad_maximum_fusion.3), channel_id=1, source_target_pairs={{0,1},{1,2},{2,3},{3,0},{4,5},{5,6},{6,7},{7,4},{8,9},{9,10},{10,1... | collective-permute-start | bytes 1966088 | tf_op jit(solution)/shard_map/ppermute | solution.py:381
  (17 other events, 138.0 us)

commit v3 on v2

--- a/solution.py
+++ b/solution.py
@@ -203,9 +203,11 @@
     q = jnp.concatenate([q_ref[...], qm_ref[...]], axis=1)
     tiles = []
     for kv_ref, bk in zip(kv_refs, sizes):
-        for j in range(0, kv_ref.shape[0], bk):
-            tiles.append((kv_ref, slice(j, j + bk), bk, first_block))
-            first_block += bk // BLOCK
+        j = 0
+        for size in bk * (kv_ref.shape[0] // sum(bk)):
+            tiles.append((kv_ref, slice(j, j + size), size, first_block))
+            first_block += size // BLOCK
+            j += size
 
     def score(tile):
         kv_ref, at, bk, block = tile
@@ -300,7 +302,7 @@
         return own, near, far
 
     early_ids, late_ids = ring_order(early), ring_order(late)
-    keys = sum(early_ids, []) + sum(late_ids, [])
+    keys = early_ids[0] + early_ids[1] + late_ids[0] + late_ids[1] + early_ids[2] + late_ids[2]
     key_ids = jnp.stack([block_id(*k) for k in keys])
     query_ids = jnp.stack(
         [block_id(y, s, g, odd) for s in (0, 1) for odd in (0, 1) for g in range(4)]
@@ -348,15 +350,16 @@
     q2, kv2, give2 = project_stage(where, w, scale, [a0, a1], [b0, b1], (3, 3), None, part, True)
     give2, kv1_near = hold((give2, kv1_near))
     q2x, kv2 = swap(kv2, give2)
+    kv2_near = near_y(kv2)
+    q = jnp.concatenate([q1, q2, q1x, q2x], axis=0)
+    q, kv1_near = hold((q, kv1_near))
     kv1_far = far_y(*kv1_near)
-    kv2_near = near_y(kv2)
     kv2_far = far_y(*kv2_near)
 
-    q = jnp.concatenate([q1, q2, q1x, q2x], axis=0)
-    state = attention(q, bias, [kv1] + kv1_near, (768,) * 3, 0, None, False)
-    state = attention(q, bias, kv1_far + [kv2], (384, 384, 640), 18, state, False)
-    state = attention(q, bias, kv2_near, (640, 640), 34, state, False)
-    out = attention(q, bias, kv2_far, (640, 640), 54, state, True)
+    big = (512, 512, 256)
+    state = attention(q, bias, [kv1] + kv1_near + [kv2], ((768,),) * 3 + (big,), 0, None, False)
+    state = attention(q, bias, kv2_near + kv1_far, (big, big, (384,), (384,)), 28, state, False)
+    out = attention(q, bias, kv2_far, ((384, 256),) * 2, 54, state, True)
 
     out = out.reshape(2, 2, nu, half, HD)
     other = pp(out[1], "blk", core_swap(nb))

time: 167 us -> 167 us (level)
  Pallas kernels: 47.7 us -> 44.7 us
  waiting for transfers between devices: 51.8 us -> 54.3 us
    pallas_call x4 -> x3, Pallas kernels: 24.5 us -> 21.5 us  [attention(): pl.pallas_call(functools.partial(attn_kernel, sizes, first_block, begin,...]
    ppermute x2, waiting for transfers between devices: 1.57 us -> 3.42 us  [swap(): got = pp(give, 'blk', core_swap(nb))]
  transfers between devices with their start and end apart: 32 -> 32, of which waited for: 13 -> 16; matrix products, arithmetic and copies ran while one was open for 5% -> 5% of each run, Pallas kernels for 25% -> 24%
where the time goes in v3:
time: 167 us
  waiting for transfers between devices  54.3 us (33%)
  starting transfers between devices  49.5 us (30%)
  Pallas kernels  44.7 us (27%)
  local copies, waits for them, and re-layouts  11.1 us (7%)
  other arithmetic  3.77 us (2%)
  between operations  3.05 us (2%)
    pallas_call x3, Pallas kernels, attention(): pl.pallas_call(functools.partial(attn_kernel, sizes, first_block, begin,...  21.5 us
    ppermute x1, waiting for transfers between devices, local(): a_m = pp(a_own, 'ulysses', ring(nu, 1))  13.5 us
    ppermute x6, starting transfers between devices, direct(): return [value] + [pp(value, axis, ring(n, s)) for s in (1, -1, 2)]  11.8 us
    pallas_call x3, Pallas kernels, project_stage(): pl.pallas_call(functools.partial(stage_kernel, len(a_parts), b_slices, in...  9.74 us
    ppermute x1, waiting for transfers between devices, local(): from_p = pp(to_m, 'tensor', ring(nt, -1))  9.09 us
    ppermute x4, starting transfers between devices, near_y(): return [pp(kv, 'blk', y_ring(nb, s)) for s in (1, -1)]  7.81 us
    ppermute x6, waiting for transfers between devices, direct(): return [value] + [pp(value, axis, ring(n, s)) for s in (1, -1, 2)]  6.62 us
    ppermute x2, starting transfers between devices, far_y(): pp(kv_p[h:], 'blk', y_ring(nb, -1))  6.12 us
  transfers between devices with their start and end apart: 32, of which 16 were waited for; matrix products, arithmetic and copies ran while one was open for 5% of the time, Pallas kernels for 24%

profile of v3, /device:TPU:0, one launch (start us, length us, event | category | flops | bytes accessed | tf_op | source)
XLA Modules:
  0.0 166.7 jit_solution(1383485293196694779)
XLA Ops:
  1.1 3.2 %collective-permute-start.2 = (bf16[128,1280]{1,0:T(8,128)(2,1)S(1)}, bf16[128,1280]{1,0:T(8,128)(2,1)S(1)}, u32[]{:S(2)}, u32[]{:S(2)}) collective-permute-start(bf16[128,1280]{1,0:T(8,128)(2,1)S(1)} %get-tuple-element.64), channel_id=1, source_target_pairs={{0,2},{1,3},{2,0},{3,1},{4,6},{5,7},{6,4},{7,5},{8,10},{9,11},{10,... | collective-permute-start | bytes 983048 | tf_op jit(solution)/shard_map/ppermute | solution.py:281
  6.3 3.9 %collective-permute-start.5 = (bf16[128,1280]{1,0:T(8,128)(2,1)S(1)}, bf16[128,1280]{1,0:T(8,128)(2,1)S(1)}, u32[]{:S(2)}, u32[]{:S(2)}) collective-permute-start(bf16[128,1280]{1,0:T(8,128)(2,1)S(1)} %get-tuple-element.63), channel_id=1, source_target_pairs={{0,64},{32,96},{64,0},{96,32},{1,65},{33,97},{65,1},{97,33},{2,66}... | collective-permute-start | bytes 983048 | tf_op jit(solution)/shard_map/ppermute | solution.py:281
  11.0 2.4 %collective-permute-done.2 = bf16[128,1280]{1,0:T(8,128)(2,1)S(1)} collective-permute-done((bf16[128,1280]{1,0:T(8,128)(2,1)S(1)}, bf16[128,1280]{1,0:T(8,128)(2,1)S(1)}, u32[]{:S(2)}, u32[]{:S(2)}) %collective-permute-start.2) | collective-permute-done | bytes 327712 | tf_op jit(solution)/shard_map/ppermute | solution.py:281
  15.4 4.0 %collective-permute-done.1 = bf16[128,1280]{1,0:T(8,128)(2,1)S(1)} collective-permute-done((bf16[128,1280]{1,0:T(8,128)(2,1)S(1)}, bf16[128,1280]{1,0:T(8,128)(2,1)S(1)}, u32[]{:S(2)}, u32[]{:S(2)}) %collective-permute-start.1) | collective-permute-done | bytes 327712 | tf_op jit(solution)/shard_map/ppermute | solution.py:281
  34.2 3.2 %copy-done = bf16[5120,3,256]{2,0,1:T(8,128)(2,1)S(1)} copy-done((bf16[5120,3,256]{2,0,1:T(8,128)(2,1)S(1)}, bf16[5120,3,256]{2,0,1:T(8,128)(2,1)}, u32[]{:S(2)}) %copy-start) | copy-done | bytes 7864344
  37.4 2.8 %shard_map.73 = (f32[128,768]{1,0:T(8,128)S(1)}, f32[512,768]{1,0:T(8,128)S(1)}) custom-call(s32[9]{0:T(128)S(1)} %pad_add_fusion.where_ref, bf16[3,5120,256]{2,1,0:T(8,128)(2,1)S(1)} %bitcast.87, f32[1,768]{1,0:T(1,128)S(1)} %bitcast.98, bf16[128,5120]{1,0:T(8,128)(2,1)S(1)} %pad_maximum_fusion.refs_0_, bf16[512,1280]{1,0:T(8,128)(2,1)S(1)} %pad_maximum_fusion.1.refs_1_), custom_call_target="tpu_custom_call" | custom-call | flops 2013265920 | bytes 7864320 | tf_op jit(solution)/shard_map/pallas_call | solution.py:152
  40.2 13.5 %collective-permute-done.6.refs_0_ = bf16[128,5120]{1,0:T(8,128)(2,1)} collective-permute-done((bf16[128,5120]{1,0:T(8,128)(2,1)S(1)}, bf16[128,5120]{1,0:T(8,128)(2,1)}, u32[]{:S(2)}, u32[]{:S(2)}) %collective-permute-start.6) | collective-permute-done | bytes 1310752 | tf_op jit(solution)/shard_map/ppermute | solution.py:322
  56.5 3.0 %collective-permute-start.9 = (bf16[64,5120]{1,0:T(8,128)(2,1)S(1)}, bf16[64,5120]{1,0:T(8,128)(2,1)S(1)}, u32[]{:S(2)}, u32[]{:S(2)}) collective-permute-start(bf16[64,5120]{1,0:T(8,128)(2,1)S(1)} %slice.88), channel_id=1, source_target_pairs={{0,96},{32,0},{64,32},{96,64},{1,97},{33,1},{65,33},{97,65},{2,98}... | collective-permute-start | bytes 1966088 | tf_op jit(solution)/shard_map/ppermute | solution.py:330
  65.1 4.0 %shard_map.74 = (bf16[384,128]{1,0:T(8,128)(2,1)S(1)}, bf16[384,256]{1,0:T(8,128)(2,1)S(1)}, bf16[384,384]{1,0:T(8,128)(2,1)S(1)}) custom-call(s32[9]{0:T(128)S(1)} %pad_add_fusion.where_ref, bf16[3,5120,256]{2,1,0:T(8,128)(2,1)S(1)} %bitcast.88, f32[1,768]{1,0:T(1,128)S(1)} %bitcast.99, bf16[128,5120]{1,0:T(8,128)(2,1)} %collective-permute-done.6.refs_0_, ...), custom_call_target="tpu_custom_call" | custom-call | flops 2013265920 | bytes 7864320 | tf_op jit(solution)/shard_map/pallas_call | solution.py:152
  72.5 2.8 %collective-permute-start.16 = (bf16[768,256]{1,0:T(8,128)(2,1)S(1)}, bf16[768,256]{1,0:T(8,128)(2,1)S(1)}, u32[]{:S(2)}, u32[]{:S(2)}) collective-permute-start(bf16[768,256]{1,0:T(8,128)(2,1)S(1)} %pad_maximum_fusion.6.refs_0_), channel_id=1, source_target_pairs={{0,24},{4,28},{8,0},{12,4},{16,8},{20,12},{24,16},{28,20},{1,25},{... | collective-permute-start | bytes 1179656 | tf_op jit(solution)/shard_map/ppermute | solution.py:339
  75.3 3.9 %shard_map.75.refs_4_ = f32[512,768]{1,0:T(8,128)S(1)} custom-call(s32[9]{0:T(128)S(1)} %pad_add_fusion.where_ref, bf16[3,5120,256]{2,1,0:T(8,128)(2,1)S(1)} %bitcast.89, f32[512,768]{1,0:T(8,128)S(1)} %get-tuple-element.41.part_ref, bf16[512,1280]{1,0:T(8,128)(2,1)} %collective-permute-done.10.refs_0_, bf16[512,1280]{1,0:T(8,128)(2,1)} %collective-permute-done.12.refs_1_), custom_call_target="tpu_custom_call" | custom-call | flops 2013265920 | bytes 3932160 | tf_op jit(solution)/shard_map/pallas_call | solution.py:124
  79.3 2.9 %shard_map.76 = (bf16[640,128]{1,0:T(8,128)(2,1)S(1)}, bf16[640,256]{1,0:T(8,128)(2,1)S(1)}, bf16[640,384]{1,0:T(8,128)(2,1)S(1)}) custom-call(s32[9]{0:T(128)S(1)} %pad_add_fusion.where_ref, bf16[3,5120,256]{2,1,0:T(8,128)(2,1)S(1)} %bitcast.90, f32[1,768]{1,0:T(1,128)S(1)} %bitcast.100, bf16[64,5120]{1,0:T(8,128)(2,1)S(1)} %collective-permute-done.8.refs_0_, ...), custom_call_target="tpu_custom_call" | custom-call | flops 2013265920 | bytes 7864320 | tf_op jit(solution)/shard_map/pallas_call | solution.py:152
  89.1 3.0 %collective-permute-start.21 = (bf16[384,256]{1,0:T(8,128)(2,1)S(1)}, bf16[384,256]{1,0:T(8,128)(2,1)S(1)}, u32[]{:S(2)}, u32[]{:S(2)}) collective-permute-start(bf16[384,256]{1,0:T(8,128)(2,1)S(1)} %slice.75), channel_id=1, source_target_pairs={{0,24},{4,28},{8,0},{12,4},{16,8},{20,12},{24,16},{28,20},{1,25},{... | collective-permute-start | bytes 589832 | tf_op jit(solution)/shard_map/ppermute | solution.py:343
  92.1 8.9 %shard_map.77 = (f32[2048,128]{1,0:T(8,128)S(1)}, f32[2048,128]{1,0:T(8,128)S(1)}, f32[2048,128]{1,0:T(8,128)S(1)}) custom-call(bf16[2048,128]{1,0:T(8,128)(2,1)S(1)} %pad_maximum_fusion.5.q_ref, bf16[2048,128]{1,0:T(8,128)(2,1)S(1)} %bitcast.95, bf16[768,256]{1,0:T(8,128)(2,1)S(1)} %pad_maximum_fusion.6.refs_0_, ...), custom_call_target="tpu_custom_call" | custom-call | flops 7516192768 | bytes 1835008 | tf_op jit(solution)/shard_map/pallas_call | solution.py:257
  101.0 3.1 %collective-permute-done.18.refs_3_ = bf16[1280,256]{1,0:T(8,128)(2,1)S(1)} collective-permute-done((bf16[1280,256]{1,0:T(8,128)(2,1)S(1)}, bf16[1280,256]{1,0:T(8,128)(2,1)S(1)}, u32[]{:S(2)}, u32[]{:S(2)}) %collective-permute-start.18) | collective-permute-done | bytes 655392 | tf_op jit(solution)/shard_map/ppermute | solution.py:339
  104.6 3.1 %collective-permute-start.23 = (bf16[640,256]{1,0:T(8,128)(2,1)S(1)}, bf16[640,256]{1,0:T(8,128)(2,1)S(1)}, u32[]{:S(2)}, u32[]{:S(2)}) collective-permute-start(bf16[640,256]{1,0:T(8,128)(2,1)S(1)} %slice.96), channel_id=1, source_target_pairs={{0,24},{4,28},{8,0},{12,4},{16,8},{20,12},{24,16},{28,20},{1,25},{... | collective-permute-start | bytes 983048 | tf_op jit(solution)/shard_map/ppermute | solution.py:343
  108.8 8.8 %shard_map.78 = (f32[2048,128]{1,0:T(8,128)S(1)}, f32[2048,128]{1,0:T(8,128)S(1)}, f32[2048,128]{1,0:T(8,128)S(1)}) custom-call(bf16[2048,128]{1,0:T(8,128)(2,1)S(1)} %pad_maximum_fusion.5.q_ref, bf16[2048,128]{1,0:T(8,128)(2,1)S(1)} %bitcast.96, f32[2048,128]{1,0:T(8,128)S(1)} %get-tuple-element.53.refs_0_, f32[2048,128]{1,0:T(8,128)S(1)} %get-tuple-element.54.refs_1_, ...), custom_call_target="tpu_custom_call" | custom-call | flops 6979321856 | bytes 1703936 | tf_op jit(solution)/shard_map/pallas_call | solution.py:257
  117.6 3.9 %shard_map.79 = bf16[2048,128]{1,0:T(8,128)(2,1)S(1)} custom-call(bf16[2048,128]{1,0:T(8,128)(2,1)S(1)} %pad_maximum_fusion.5.q_ref, bf16[2048,128]{1,0:T(8,128)(2,1)S(1)} %bitcast.97, f32[2048,128]{1,0:T(8,128)S(1)} %get-tuple-element.56.refs_0_, f32[2048,128]{1,0:T(8,128)S(1)} %get-tuple-element.57.refs_1_, f32[2048,128]{1,0:T(8,128)S(1)} %get-tuple-element.58.refs_2_, ...), custom_call_target="tpu_custom_call" | custom-call | flops 2684354560 | bytes 655360 | tf_op jit(solution)/shard_map/pallas_call | solution.py:257
  126.8 4.7 %shard_map.80.refs_4_ = bf16[4,4,256,1280]{3,2,1,0:T(8,128)(2,1)S(1)} custom-call(s32[9]{0:T(128)S(1)} %pad_add_fusion.where_ref, bf16[256,256]{1,0:T(8,128)(2,1)S(1)} %bitcast.91, bf16[4,256,5120]{2,1,0:T(8,128)(2,1)} %hbm.1), custom_call_target="tpu_custom_call" | custom-call | bytes 20971520 | tf_op jit(solution)/shard_map/pallas_call | solution.py:65
  131.5 3.0 %collective-permute-done.26.refs_2_ = bf16[256,256]{1,0:T(8,128)(2,1)S(1)} collective-permute-done((bf16[256,256]{1,0:T(8,128)(2,1)S(1)}, bf16[256,256]{1,0:T(8,128)(2,1)S(1)}, u32[]{:S(2)}, u32[]{:S(2)}) %collective-permute-start.26) | collective-permute-done | bytes 131104 | tf_op jit(solution)/shard_map/ppermute | solution.py:372
  140.3 4.6 %collective-permute-done.30 = bf16[128,1280]{1,0:T(8,128)(2,1)S(1)} collective-permute-done((bf16[128,1280]{1,0:T(8,128)(2,1)S(1)}, bf16[128,1280]{1,0:T(8,128)(2,1)S(1)}, u32[]{:S(2)}, u32[]{:S(2)}) %collective-permute-start.30) | collective-permute-done | bytes 327712 | tf_op jit(solution)/shard_map/ppermute | solution.py:380
  145.0 2.7 %collective-permute-start.31 = (bf16[256,1280]{1,0:T(8,128)(2,1)S(1)}, bf16[256,1280]{1,0:T(8,128)(2,1)S(1)}, u32[]{:S(2)}, u32[]{:S(2)}) collective-permute-start(bf16[256,1280]{1,0:T(8,128)(2,1)S(1)} %pad_maximum_fusion.4), channel_id=1, source_target_pairs={{0,3},{1,0},{2,1},{3,2},{4,7},{5,4},{6,5},{7,6},{8,11},{9,8},{10,9... | collective-permute-start | bytes 1966088 | tf_op jit(solution)/shard_map/ppermute | solution.py:385
  151.1 9.1 %collective-permute-done.31 = bf16[256,1280]{1,0:T(8,128)(2,1)S(1)} collective-permute-done((bf16[256,1280]{1,0:T(8,128)(2,1)S(1)}, bf16[256,1280]{1,0:T(8,128)(2,1)S(1)}, u32[]{:S(2)}, u32[]{:S(2)}) %collective-permute-start.31) | collective-permute-done | bytes 655392 | tf_op jit(solution)/shard_map/ppermute | solution.py:385
  160.2 5.4 %collective-permute-done.29 = bf16[256,1280]{1,0:T(8,128)(2,1)S(1)} collective-permute-done((bf16[256,1280]{1,0:T(8,128)(2,1)S(1)}, bf16[256,1280]{1,0:T(8,128)(2,1)S(1)}, u32[]{:S(2)}, u32[]{:S(2)}) %collective-permute-start.29) | collective-permute-done | bytes 655392 | tf_op jit(solution)/shard_map/ppermute | solution.py:384
  (111 shorter events, 53.7 us)
Async XLA Ops:
  1.1 12.2 %collective-permute-start.2 = (bf16[128,1280]{1,0:T(8,128)(2,1)S(1)}, bf16[128,1280]{1,0:T(8,128)(2,1)S(1)}, u32[]{:S(2)}, u32[]{:S(2)}) collective-permute-start(bf16[128,1280]{1,0:T(8,128)(2,1)S(1)} %get-tuple-element.64), channel_id=1, source_target_pairs={{0,2},{1,3},{2,0},{3,1},{4,6},{5,7},{6,4},{7,5},{8,10},{9,11},{10,... | collective-permute-start | bytes 983048 | tf_op jit(solution)/shard_map/ppermute | solution.py:281
  4.3 15.1 %collective-permute-start.1 = (bf16[128,1280]{1,0:T(8,128)(2,1)S(1)}, bf16[128,1280]{1,0:T(8,128)(2,1)S(1)}, u32[]{:S(2)}, u32[]{:S(2)}) collective-permute-start(bf16[128,1280]{1,0:T(8,128)(2,1)S(1)} %get-tuple-element.64), channel_id=1, source_target_pairs={{0,3},{1,0},{2,1},{3,2},{4,7},{5,4},{6,5},{7,6},{8,11},{9,8},{10,9... | collective-permute-start | bytes 983048 | tf_op jit(solution)/shard_map/ppermute | solution.py:281
  5.5 13.9 %collective-permute-start = (bf16[128,1280]{1,0:T(8,128)(2,1)S(1)}, bf16[128,1280]{1,0:T(8,128)(2,1)}, u32[]{:S(2)}, u32[]{:S(2)}) collective-permute-start(bf16[128,1280]{1,0:T(8,128)(2,1)S(1)} %get-tuple-element.64), channel_id=1, source_target_pairs={{0,1},{1,2},{2,3},{3,0},{4,5},{5,6},{6,7},{7,4},{8,9},{9,10},{10,1... | collective-permute-start | bytes 983048 | tf_op jit(solution)/shard_map/ppermute | solution.py:281
  6.3 18.4 %collective-permute-start.5 = (bf16[128,1280]{1,0:T(8,128)(2,1)S(1)}, bf16[128,1280]{1,0:T(8,128)(2,1)S(1)}, u32[]{:S(2)}, u32[]{:S(2)}) collective-permute-start(bf16[128,1280]{1,0:T(8,128)(2,1)S(1)} %get-tuple-element.63), channel_id=1, source_target_pairs={{0,64},{32,96},{64,0},{96,32},{1,65},{33,97},{65,1},{97,33},{2,66}... | collective-permute-start | bytes 983048 | tf_op jit(solution)/shard_map/ppermute | solution.py:281
  10.2 14.7 %collective-permute-start.4 = (bf16[128,1280]{1,0:T(8,128)(2,1)S(1)}, bf16[128,1280]{1,0:T(8,128)(2,1)S(1)}, u32[]{:S(2)}, u32[]{:S(2)}) collective-permute-start(bf16[128,1280]{1,0:T(8,128)(2,1)S(1)} %get-tuple-element.63), channel_id=1, source_target_pairs={{0,96},{32,0},{64,32},{96,64},{1,97},{33,1},{65,33},{97,65},{2,98}... | collective-permute-start | bytes 983048 | tf_op jit(solution)/shard_map/ppermute | solution.py:281
  13.4 12.2 %collective-permute-start.3 = (bf16[128,1280]{1,0:T(8,128)(2,1)S(1)}, bf16[128,1280]{1,0:T(8,128)(2,1)S(1)}, u32[]{:S(2)}, u32[]{:S(2)}) collective-permute-start(bf16[128,1280]{1,0:T(8,128)(2,1)S(1)} %get-tuple-element.63), channel_id=1, source_target_pairs={{0,32},{32,64},{64,96},{96,0},{1,33},{33,65},{65,97},{97,1},{2,34}... | collective-permute-start | bytes 983048 | tf_op jit(solution)/shard_map/ppermute | solution.py:281
  20.6 33.1 %collective-permute-start.6 = (bf16[128,5120]{1,0:T(8,128)(2,1)S(1)}, bf16[128,5120]{1,0:T(8,128)(2,1)}, u32[]{:S(2)}, u32[]{:S(2)}) collective-permute-start(bf16[128,5120]{1,0:T(8,128)(2,1)S(1)} %pad_maximum_fusion.refs_0_), channel_id=1, source_target_pairs={{0,32},{32,64},{64,96},{96,0},{1,33},{33,65},{65,97},{97,1},{2,34}... | collective-permute-start | bytes 3932168 | tf_op jit(solution)/shard_map/ppermute | solution.py:322
  22.5 32.8 %collective-permute-start.7 = (bf16[128,5120]{1,0:T(8,128)(2,1)S(1)}, bf16[128,5120]{1,0:T(8,128)(2,1)}, u32[]{:S(2)}, u32[]{:S(2)}) collective-permute-start(bf16[128,5120]{1,0:T(8,128)(2,1)S(1)} %pad_maximum_fusion.refs_0_), channel_id=1, source_target_pairs={{0,96},{32,0},{64,32},{96,64},{1,97},{33,1},{65,33},{97,65},{2,98}... | collective-permute-start | bytes 3932168 | tf_op jit(solution)/shard_map/ppermute | solution.py:324
  26.7 32.7 %collective-permute-start.10 = (bf16[512,1280]{1,0:T(8,128)(2,1)S(1)}, bf16[512,1280]{1,0:T(8,128)(2,1)}, u32[]{:S(2)}, u32[]{:S(2)}) collective-permute-start(bf16[512,1280]{1,0:T(8,128)(2,1)S(1)} %pad_maximum_fusion.1.refs_1_), channel_id=1, source_target_pairs={{0,1},{1,2},{2,3},{3,0},{4,5},{5,6},{6,7},{7,4},{8,9},{9,10},{10,1... | collective-permute-start | bytes 3932168 | tf_op jit(solution)/shard_map/ppermute | solution.py:323
  28.1 34.0 %collective-permute-start.12 = (bf16[512,1280]{1,0:T(8,128)(2,1)S(1)}, bf16[512,1280]{1,0:T(8,128)(2,1)}, u32[]{:S(2)}, u32[]{:S(2)}) collective-permute-start(bf16[512,1280]{1,0:T(8,128)(2,1)S(1)} %pad_maximum_fusion.1.refs_1_), channel_id=1, source_target_pairs={{0,3},{1,0},{2,1},{3,2},{4,7},{5,4},{6,5},{7,6},{8,11},{9,8},{10,9... | collective-permute-start | bytes 3932168 | tf_op jit(solution)/shard_map/ppermute | solution.py:325
  54.9 17.6 %collective-permute-start.8 = (bf16[64,5120]{1,0:T(8,128)(2,1)S(1)}, bf16[64,5120]{1,0:T(8,128)(2,1)S(1)}, u32[]{:S(2)}, u32[]{:S(2)}) collective-permute-start(bf16[64,5120]{1,0:T(8,128)(2,1)S(1)} %slice.66), channel_id=1, source_target_pairs={{0,32},{32,64},{64,96},{96,0},{1,33},{33,65},{65,97},{97,1},{2,34}... | collective-permute-start | bytes 1966088 | tf_op jit(solution)/shard_map/ppermute | solution.py:329
  56.5 22.8 %collective-permute-start.9 = (bf16[64,5120]{1,0:T(8,128)(2,1)S(1)}, bf16[64,5120]{1,0:T(8,128)(2,1)S(1)}, u32[]{:S(2)}, u32[]{:S(2)}) collective-permute-start(bf16[64,5120]{1,0:T(8,128)(2,1)S(1)} %slice.88), channel_id=1, source_target_pairs={{0,96},{32,0},{64,32},{96,64},{1,97},{33,1},{65,33},{97,65},{2,98}... | collective-permute-start | bytes 1966088 | tf_op jit(solution)/shard_map/ppermute | solution.py:330
  60.6 18.7 %collective-permute-start.11 = (bf16[256,1280]{1,0:T(8,128)(2,1)S(1)}, bf16[256,1280]{1,0:T(8,128)(2,1)S(1)}, u32[]{:S(2)}, u32[]{:S(2)}) collective-permute-start(bf16[256,1280]{1,0:T(8,128)(2,1)S(1)} %slice.89), channel_id=1, source_target_pairs={{0,1},{1,2},{2,3},{3,0},{4,5},{5,6},{6,7},{7,4},{8,9},{9,10},{10,1... | collective-permute-start | bytes 1966088 | tf_op jit(solution)/shard_map/ppermute | solution.py:331
  63.3 16.0 %collective-permute-start.13 = (bf16[256,1280]{1,0:T(8,128)(2,1)S(1)}, bf16[256,1280]{1,0:T(8,128)(2,1)S(1)}, u32[]{:S(2)}, u32[]{:S(2)}) collective-permute-start(bf16[256,1280]{1,0:T(8,128)(2,1)S(1)} %slice.90), channel_id=1, source_target_pairs={{0,3},{1,0},{2,1},{3,2},{4,7},{5,4},{6,5},{7,6},{8,11},{9,8},{10,9... | collective-permute-start | bytes 1966088 | tf_op jit(solution)/shard_map/ppermute | solution.py:332
  70.8 12.5 %collective-permute-start.15 = (bf16[768,256]{1,0:T(8,128)(2,1)S(1)}, bf16[768,256]{1,0:T(8,128)(2,1)S(1)}, u32[]{:S(2)}, u32[]{:S(2)}) collective-permute-start(bf16[768,256]{1,0:T(8,128)(2,1)S(1)} %pad_maximum_fusion.6.refs_0_), channel_id=1, source_target_pairs={{0,8},{4,12},{8,16},{12,20},{16,24},{20,28},{24,0},{28,4},{1,9},{5... | collective-permute-start | bytes 1179656 | tf_op jit(solution)/shard_map/ppermute | solution.py:339
  72.5 10.9 %collective-permute-start.16 = (bf16[768,256]{1,0:T(8,128)(2,1)S(1)}, bf16[768,256]{1,0:T(8,128)(2,1)S(1)}, u32[]{:S(2)}, u32[]{:S(2)}) collective-permute-start(bf16[768,256]{1,0:T(8,128)(2,1)S(1)} %pad_maximum_fusion.6.refs_0_), channel_id=1, source_target_pairs={{0,24},{4,28},{8,0},{12,4},{16,8},{20,12},{24,16},{28,20},{1,25},{... | collective-permute-start | bytes 1179656 | tf_op jit(solution)/shard_map/ppermute | solution.py:339
  85.3 18.8 %collective-permute-start.18 = (bf16[1280,256]{1,0:T(8,128)(2,1)S(1)}, bf16[1280,256]{1,0:T(8,128)(2,1)S(1)}, u32[]{:S(2)}, u32[]{:S(2)}) collective-permute-start(bf16[1280,256]{1,0:T(8,128)(2,1)S(1)} %pad_maximum_fusion.2.refs_3_), channel_id=1, source_target_pairs={{0,8},{4,12},{8,16},{12,20},{16,24},{20,28},{24,0},{28,4},{1,9},{5... | collective-permute-start | bytes 1966088 | tf_op jit(solution)/shard_map/ppermute | solution.py:339
  86.9 17.7 %collective-permute-start.19 = (bf16[1280,256]{1,0:T(8,128)(2,1)S(1)}, bf16[1280,256]{1,0:T(8,128)(2,1)S(1)}, u32[]{:S(2)}, u32[]{:S(2)}) collective-permute-start(bf16[1280,256]{1,0:T(8,128)(2,1)S(1)} %pad_maximum_fusion.2.refs_3_), channel_id=1, source_target_pairs={{0,24},{4,28},{8,0},{12,4},{16,8},{20,12},{24,16},{28,20},{1,25},{... | collective-permute-start | bytes 1966088 | tf_op jit(solution)/shard_map/ppermute | solution.py:339
  88.7 19.6 %collective-permute-start.20 = (bf16[384,256]{1,0:T(8,128)(2,1)S(1)}, bf16[384,256]{1,0:T(8,128)(2,1)S(1)}, u32[]{:S(2)}, u32[]{:S(2)}) collective-permute-start(bf16[384,256]{1,0:T(8,128)(2,1)S(1)} %slice.74), channel_id=1, source_target_pairs={{0,8},{4,12},{8,16},{12,20},{16,24},{20,28},{24,0},{28,4},{1,9},{5... | collective-permute-start | bytes 589832 | tf_op jit(solution)/shard_map/ppermute | solution.py:343
  89.1 19.6 %collective-permute-start.21 = (bf16[384,256]{1,0:T(8,128)(2,1)S(1)}, bf16[384,256]{1,0:T(8,128)(2,1)S(1)}, u32[]{:S(2)}, u32[]{:S(2)}) collective-permute-start(bf16[384,256]{1,0:T(8,128)(2,1)S(1)} %slice.75), channel_id=1, source_target_pairs={{0,24},{4,28},{8,0},{12,4},{16,8},{20,12},{24,16},{28,20},{1,25},{... | collective-permute-start | bytes 589832 | tf_op jit(solution)/shard_map/ppermute | solution.py:343
  104.1 13.4 %collective-permute-start.22 = (bf16[640,256]{1,0:T(8,128)(2,1)S(1)}, bf16[640,256]{1,0:T(8,128)(2,1)S(1)}, u32[]{:S(2)}, u32[]{:S(2)}) collective-permute-start(bf16[640,256]{1,0:T(8,128)(2,1)S(1)} %slice.95), channel_id=1, source_target_pairs={{0,8},{4,12},{8,16},{12,20},{16,24},{20,28},{24,0},{28,4},{1,9},{5... | collective-permute-start | bytes 983048 | tf_op jit(solution)/shard_map/ppermute | solution.py:343
  104.6 12.9 %collective-permute-start.23 = (bf16[640,256]{1,0:T(8,128)(2,1)S(1)}, bf16[640,256]{1,0:T(8,128)(2,1)S(1)}, u32[]{:S(2)}, u32[]{:S(2)}) collective-permute-start(bf16[640,256]{1,0:T(8,128)(2,1)S(1)} %slice.96), channel_id=1, source_target_pairs={{0,24},{4,28},{8,0},{12,4},{16,8},{20,12},{24,16},{28,20},{1,25},{... | collective-permute-start | bytes 983048 | tf_op jit(solution)/shard_map/ppermute | solution.py:343
  145.0 15.2 %collective-permute-start.31 = (bf16[256,1280]{1,0:T(8,128)(2,1)S(1)}, bf16[256,1280]{1,0:T(8,128)(2,1)S(1)}, u32[]{:S(2)}, u32[]{:S(2)}) collective-permute-start(bf16[256,1280]{1,0:T(8,128)(2,1)S(1)} %pad_maximum_fusion.4), channel_id=1, source_target_pairs={{0,3},{1,0},{2,1},{3,2},{4,7},{5,4},{6,5},{7,6},{8,11},{9,8},{10,9... | collective-permute-start | bytes 1966088 | tf_op jit(solution)/shard_map/ppermute | solution.py:385
  149.6 16.0 %collective-permute-start.29 = (bf16[256,1280]{1,0:T(8,128)(2,1)S(1)}, bf16[256,1280]{1,0:T(8,128)(2,1)S(1)}, u32[]{:S(2)}, u32[]{:S(2)}) collective-permute-start(bf16[256,1280]{1,0:T(8,128)(2,1)S(1)} %pad_maximum_fusion.3), channel_id=1, source_target_pairs={{0,1},{1,2},{2,3},{3,0},{4,5},{5,6},{6,7},{7,4},{8,9},{9,10},{10,1... | collective-permute-start | bytes 1966088 | tf_op jit(solution)/shard_map/ppermute | solution.py:384
  (17 other events, 135.4 us)

commit v4 on v3

--- a/solution.py
+++ b/solution.py
@@ -352,12 +352,12 @@
     q2x, kv2 = swap(kv2, give2)
     kv2_near = near_y(kv2)
     q = jnp.concatenate([q1, q2, q1x, q2x], axis=0)
-    q, kv1_near = hold((q, kv1_near))
-    kv1_far = far_y(*kv1_near)
     kv2_far = far_y(*kv2_near)
 
     big = (512, 512, 256)
     state = attention(q, bias, [kv1] + kv1_near + [kv2], ((768,),) * 3 + (big,), 0, None, False)
+    state, kv1_near = hold((state, kv1_near))
+    kv1_far = far_y(*kv1_near)
     state = attention(q, bias, kv2_near + kv1_far, (big, big, (384,), (384,)), 28, state, False)
     out = attention(q, bias, kv2_far, ((384, 256),) * 2, 54, state, True)
 
@@ -378,7 +378,8 @@
     hr = rows // 2
     far_m = pp(far_0, "tensor", ring(nt, 1))
     far_p = pp(far_1, "tensor", ring(nt, -1))
-    to_m, to_p = out_project(where, arrived, w_o, (1, 2), jnp.float32, 1)
+    (to_m,) = out_project(where, arrived, w_o, (1,), jnp.float32, 1)
+    (to_p,) = out_project(where, arrived, w_o, (2,), jnp.float32, 1)
     to_p = jnp.concatenate([to_p[:hr] + far_m.astype(jnp.float32), to_p[hr:]], axis=0).astype(bf)
     to_m = jnp.concatenate([to_m[:hr], to_m[hr:] + far_p.astype(jnp.float32)], axis=0).astype(bf)
     from_m = pp(to_p, "tensor", ring(nt, 1))

time: 167 us -> 175 us (1.048)
  waiting for transfers between devices: 54.3 us -> 65.1 us
  starting transfers between devices: 49.5 us -> 45.7 us
    ppermute x1, waiting for transfers between devices: 0.01 us -> 18.8 us  [local(): a_p = pp(a_own, 'ulysses', ring(nu, -1))]
    ppermute x1, waiting for transfers between devices: 13.5 us -> 0.01 us  [local(): a_m = pp(a_own, 'ulysses', ring(nu, 1))]
    ppermute x4, starting transfers between devices: 7.81 us -> 5.18 us  [near_y(): return [pp(kv, 'blk', y_ring(nb, s)) for s in (1, -1)]]
    ppermute x1, waiting for transfers between devices: 0.01 us -> 2.34 us  [local(): b0 = pp(b_m[:bh], 'tensor', ring(nt, 1))]
    ppermute x1, waiting for transfers between devices: 9.09 us -> 11.3 us  [local(): from_p = pp(to_m, 'tensor', ring(nt, -1))]
    ppermute x1, starting transfers between devices: 1.99 us -> 0.01 us  [local(): a_m = pp(a_own, 'ulysses', ring(nu, 1))]
    ppermute x1, starting transfers between devices: 2.2 us -> 4.11 us  [local(): a_p = pp(a_own, 'ulysses', ring(nu, -1))]
    ppermute x1, waiting for transfers between devices: 5.4 us -> 3.6 us  [local(): from_m = pp(to_p, 'tensor', ring(nt, 1))]
  transfers between devices with their start and end apart: 32 -> 32, of which waited for: 16 -> 19; matrix products, arithmetic and copies ran while one was open for 5% -> 5% of each run, Pallas kernels for 24% -> 23%
where the time goes in v4:
time: 175 us; the launch traced here: 174 us
  waiting for transfers between devices  65.1 us (37%)
  starting transfers between devices  45.7 us (26%)
  Pallas kernels  45.4 us (26%)
  local copies, waits for them, and re-layouts  11.1 us (6%)
  other arithmetic  3.76 us (2%)
  between operations  2.95 us (2%)
    pallas_call x3, Pallas kernels, attention(): pl.pallas_call(functools.partial(attn_kernel, sizes, first_block, begin,...  21.5 us
    ppermute x1, waiting for transfers between devices, local(): a_p = pp(a_own, 'ulysses', ring(nu, -1))  18.8 us
    ppermute x6, starting transfers between devices, direct(): return [value] + [pp(value, axis, ring(n, s)) for s in (1, -1, 2)]  11.8 us
    ppermute x1, waiting for transfers between devices, local(): from_p = pp(to_m, 'tensor', ring(nt, -1))  11.3 us
    pallas_call x3, Pallas kernels, project_stage(): pl.pallas_call(functools.partial(stage_kernel, len(a_parts), b_slices, in...  9.75 us
    ppermute x6, waiting for transfers between devices, direct(): return [value] + [pp(value, axis, ring(n, s)) for s in (1, -1, 2)]  8.14 us
    ppermute x2, starting transfers between devices, far_y(): pp(kv_p[h:], 'blk', y_ring(nb, -1))  5.64 us
    pallas_call x4, Pallas kernels, out_project(): pl.pallas_call(functools.partial(out_kernel, places), in_specs=[pl.BlockS...  5.56 us
  transfers between devices with their start and end apart: 32, of which 19 were waited for; matrix products, arithmetic and copies ran while one was open for 5% of the time, Pallas kernels for 23%

profile of v4, /device:TPU:0, one launch (start us, length us, event | category | flops | bytes accessed | tf_op | source)
XLA Modules:
  0.0 174.3 jit_solution(18357882611548048762)
XLA Ops:
  1.1 3.2 %collective-permute-start.2 = (bf16[128,1280]{1,0:T(8,128)(2,1)S(1)}, bf16[128,1280]{1,0:T(8,128)(2,1)S(1)}, u32[]{:S(2)}, u32[]{:S(2)}) collective-permute-start(bf16[128,1280]{1,0:T(8,128)(2,1)S(1)} %get-tuple-element.64), channel_id=1, source_target_pairs={{0,2},{1,3},{2,0},{3,1},{4,6},{5,7},{6,4},{7,5},{8,10},{9,11},{10,... | collective-permute-start | bytes 983048 | tf_op jit(solution)/shard_map/ppermute | solution.py:281
  6.3 3.9 %collective-permute-start.5 = (bf16[128,1280]{1,0:T(8,128)(2,1)S(1)}, bf16[128,1280]{1,0:T(8,128)(2,1)S(1)}, u32[]{:S(2)}, u32[]{:S(2)}) collective-permute-start(bf16[128,1280]{1,0:T(8,128)(2,1)S(1)} %get-tuple-element.63), channel_id=1, source_target_pairs={{0,64},{32,96},{64,0},{96,32},{1,65},{33,97},{65,1},{97,33},{2,66}... | collective-permute-start | bytes 983048 | tf_op jit(solution)/shard_map/ppermute | solution.py:281
  15.4 4.0 %collective-permute-done.1 = bf16[128,1280]{1,0:T(8,128)(2,1)S(1)} collective-permute-done((bf16[128,1280]{1,0:T(8,128)(2,1)S(1)}, bf16[128,1280]{1,0:T(8,128)(2,1)S(1)}, u32[]{:S(2)}, u32[]{:S(2)}) %collective-permute-start.1) | collective-permute-done | bytes 327712 | tf_op jit(solution)/shard_map/ppermute | solution.py:281
  20.6 4.1 %collective-permute-start.7 = (bf16[128,5120]{1,0:T(8,128)(2,1)S(1)}, bf16[128,5120]{1,0:T(8,128)(2,1)}, u32[]{:S(2)}, u32[]{:S(2)}) collective-permute-start(bf16[128,5120]{1,0:T(8,128)(2,1)S(1)} %pad_maximum_fusion.refs_0_), channel_id=1, source_target_pairs={{0,96},{32,0},{64,32},{96,64},{1,97},{33,1},{65,33},{97,65},{2,98}... | collective-permute-start | bytes 3932168 | tf_op jit(solution)/shard_map/ppermute | solution.py:324
  34.3 18.8 %collective-permute-done.7.refs_1_ = bf16[128,5120]{1,0:T(8,128)(2,1)} collective-permute-done((bf16[128,5120]{1,0:T(8,128)(2,1)S(1)}, bf16[128,5120]{1,0:T(8,128)(2,1)}, u32[]{:S(2)}, u32[]{:S(2)}) %collective-permute-start.7) | collective-permute-done | bytes 1310752 | tf_op jit(solution)/shard_map/ppermute | solution.py:324
  54.2 3.6 %collective-permute-start.9 = (bf16[64,5120]{1,0:T(8,128)(2,1)S(1)}, bf16[64,5120]{1,0:T(8,128)(2,1)S(1)}, u32[]{:S(2)}, u32[]{:S(2)}) collective-permute-start(bf16[64,5120]{1,0:T(8,128)(2,1)S(1)} %slice.88), channel_id=1, source_target_pairs={{0,96},{32,0},{64,32},{96,64},{1,97},{33,1},{65,33},{97,65},{2,98}... | collective-permute-start | bytes 1966088 | tf_op jit(solution)/shard_map/ppermute | solution.py:330
  57.9 3.2 %copy-done = bf16[5120,3,256]{2,0,1:T(8,128)(2,1)S(1)} copy-done((bf16[5120,3,256]{2,0,1:T(8,128)(2,1)S(1)}, bf16[5120,3,256]{2,0,1:T(8,128)(2,1)}, u32[]{:S(2)}) %copy-start) | copy-done | bytes 7864344
  61.1 2.8 %shard_map.73 = (f32[128,768]{1,0:T(8,128)S(1)}, f32[512,768]{1,0:T(8,128)S(1)}) custom-call(s32[9]{0:T(128)S(1)} %pad_add_fusion.where_ref, bf16[3,5120,256]{2,1,0:T(8,128)(2,1)S(1)} %bitcast.87, f32[1,768]{1,0:T(1,128)S(1)} %bitcast.99, bf16[128,5120]{1,0:T(8,128)(2,1)S(1)} %pad_maximum_fusion.refs_0_, bf16[512,1280]{1,0:T(8,128)(2,1)S(1)} %pad_maximum_fusion.1.refs_1_), custom_call_target="tpu_custom_call" | custom-call | flops 2013265920 | bytes 7864320 | tf_op jit(solution)/shard_map/pallas_call | solution.py:152
  70.3 4.0 %shard_map.74 = (bf16[384,128]{1,0:T(8,128)(2,1)S(1)}, bf16[384,256]{1,0:T(8,128)(2,1)S(1)}, bf16[384,384]{1,0:T(8,128)(2,1)S(1)}) custom-call(s32[9]{0:T(128)S(1)} %pad_add_fusion.where_ref, bf16[3,5120,256]{2,1,0:T(8,128)(2,1)S(1)} %bitcast.88, f32[1,768]{1,0:T(1,128)S(1)} %bitcast.100, bf16[128,5120]{1,0:T(8,128)(2,1)} %collective-permute-done.6.refs_0_, ...), custom_call_target="tpu_custom_call" | custom-call | flops 2013265920 | bytes 7864320 | tf_op jit(solution)/shard_map/pallas_call | solution.py:152
  76.0 3.1 %collective-permute-start.16 = (bf16[768,256]{1,0:T(8,128)(2,1)S(1)}, bf16[768,256]{1,0:T(8,128)(2,1)S(1)}, u32[]{:S(2)}, u32[]{:S(2)}) collective-permute-start(bf16[768,256]{1,0:T(8,128)(2,1)S(1)} %pad_maximum_fusion.6.refs_0_), channel_id=1, source_target_pairs={{0,24},{4,28},{8,0},{12,4},{16,8},{20,12},{24,16},{28,20},{1,25},{... | collective-permute-start | bytes 1179656 | tf_op jit(solution)/shard_map/ppermute | solution.py:339
  79.1 3.9 %shard_map.75.refs_4_ = f32[512,768]{1,0:T(8,128)S(1)} custom-call(s32[9]{0:T(128)S(1)} %pad_add_fusion.where_ref, bf16[3,5120,256]{2,1,0:T(8,128)(2,1)S(1)} %bitcast.89, f32[512,768]{1,0:T(8,128)S(1)} %get-tuple-element.41.part_ref, bf16[512,1280]{1,0:T(8,128)(2,1)} %collective-permute-done.10.refs_0_, bf16[512,1280]{1,0:T(8,128)(2,1)} %collective-permute-done.12.refs_1_), custom_call_target="tpu_custom_call" | custom-call | flops 2013265920 | bytes 3932160 | tf_op jit(solution)/shard_map/pallas_call | solution.py:124
  86.7 2.9 %shard_map.76 = (bf16[640,128]{1,0:T(8,128)(2,1)S(1)}, bf16[640,256]{1,0:T(8,128)(2,1)S(1)}, bf16[640,384]{1,0:T(8,128)(2,1)S(1)}) custom-call(s32[9]{0:T(128)S(1)} %pad_add_fusion.where_ref, bf16[3,5120,256]{2,1,0:T(8,128)(2,1)S(1)} %bitcast.90, f32[1,768]{1,0:T(1,128)S(1)} %bitcast.101, bf16[64,5120]{1,0:T(8,128)(2,1)S(1)} %collective-permute-done.8.refs_0_, ...), custom_call_target="tpu_custom_call" | custom-call | flops 2013265920 | bytes 7864320 | tf_op jit(solution)/shard_map/pallas_call | solution.py:152
  95.3 8.9 %shard_map.77 = (f32[2048,128]{1,0:T(8,128)S(1)}, f32[2048,128]{1,0:T(8,128)S(1)}, f32[2048,128]{1,0:T(8,128)S(1)}) custom-call(bf16[2048,128]{1,0:T(8,128)(2,1)S(1)} %pad_maximum_fusion.5.q_ref, bf16[2048,128]{1,0:T(8,128)(2,1)S(1)} %bitcast.96, bf16[768,256]{1,0:T(8,128)(2,1)S(1)} %pad_maximum_fusion.6.refs_0_, ...), custom_call_target="tpu_custom_call" | custom-call | flops 7516192768 | bytes 1835008 | tf_op jit(solution)/shard_map/pallas_call | solution.py:257
  104.3 2.8 %collective-permute-start.21 = (bf16[384,256]{1,0:T(8,128)(2,1)S(1)}, bf16[384,256]{1,0:T(8,128)(2,1)S(1)}, u32[]{:S(2)}, u32[]{:S(2)}) collective-permute-start(bf16[384,256]{1,0:T(8,128)(2,1)S(1)} %slice.75), channel_id=1, source_target_pairs={{0,24},{4,28},{8,0},{12,4},{16,8},{20,12},{24,16},{28,20},{1,25},{... | collective-permute-start | bytes 589832 | tf_op jit(solution)/shard_map/ppermute | solution.py:343
  107.1 3.7 %collective-permute-done.19.refs_4_ = bf16[1280,256]{1,0:T(8,128)(2,1)S(1)} collective-permute-done((bf16[1280,256]{1,0:T(8,128)(2,1)S(1)}, bf16[1280,256]{1,0:T(8,128)(2,1)S(1)}, u32[]{:S(2)}, u32[]{:S(2)}) %collective-permute-start.19) | collective-permute-done | bytes 655392 | tf_op jit(solution)/shard_map/ppermute | solution.py:339
  110.8 2.8 %collective-permute-start.23 = (bf16[640,256]{1,0:T(8,128)(2,1)S(1)}, bf16[640,256]{1,0:T(8,128)(2,1)S(1)}, u32[]{:S(2)}, u32[]{:S(2)}) collective-permute-start(bf16[640,256]{1,0:T(8,128)(2,1)S(1)} %slice.96), channel_id=1, source_target_pairs={{0,24},{4,28},{8,0},{12,4},{16,8},{20,12},{24,16},{28,20},{1,25},{... | collective-permute-start | bytes 983048 | tf_op jit(solution)/shard_map/ppermute | solution.py:343
  117.3 8.8 %shard_map.78 = (f32[2048,128]{1,0:T(8,128)S(1)}, f32[2048,128]{1,0:T(8,128)S(1)}, f32[2048,128]{1,0:T(8,128)S(1)}) custom-call(bf16[2048,128]{1,0:T(8,128)(2,1)S(1)} %pad_maximum_fusion.5.q_ref, bf16[2048,128]{1,0:T(8,128)(2,1)S(1)} %bitcast.97, f32[2048,128]{1,0:T(8,128)S(1)} %get-tuple-element.53.refs_0_, f32[2048,128]{1,0:T(8,128)S(1)} %get-tuple-element.54.refs_1_, ...), custom_call_target="tpu_custom_call" | custom-call | flops 6979321856 | bytes 1703936 | tf_op jit(solution)/shard_map/pallas_call | solution.py:257
  126.1 3.9 %shard_map.79 = bf16[2048,128]{1,0:T(8,128)(2,1)S(1)} custom-call(bf16[2048,128]{1,0:T(8,128)(2,1)S(1)} %pad_maximum_fusion.5.q_ref, bf16[2048,128]{1,0:T(8,128)(2,1)S(1)} %bitcast.98, f32[2048,128]{1,0:T(8,128)S(1)} %get-tuple-element.58.refs_0_, f32[2048,128]{1,0:T(8,128)S(1)} %get-tuple-element.59.refs_1_, f32[2048,128]{1,0:T(8,128)S(1)} %get-tuple-element.60.refs_2_, ...), custom_call_target="tpu_custom_call" | custom-call | flops 2684354560 | bytes 655360 | tf_op jit(solution)/shard_map/pallas_call | solution.py:257
  134.9 4.7 %shard_map.80.refs_4_ = bf16[4,4,256,1280]{3,2,1,0:T(8,128)(2,1)S(1)} custom-call(s32[9]{0:T(128)S(1)} %pad_add_fusion.where_ref, bf16[256,256]{1,0:T(8,128)(2,1)S(1)} %bitcast.91, bf16[4,256,5120]{2,1,0:T(8,128)(2,1)} %hbm.1), custom_call_target="tpu_custom_call" | custom-call | bytes 20971520 | tf_op jit(solution)/shard_map/pallas_call | solution.py:65
  143.1 3.0 %collective-permute-start.30 = (bf16[128,1280]{1,0:T(8,128)(2,1)S(1)}, bf16[128,1280]{1,0:T(8,128)(2,1)S(1)}, u32[]{:S(2)}, u32[]{:S(2)}) collective-permute-start(bf16[128,1280]{1,0:T(8,128)(2,1)S(1)} %get-tuple-element.62), channel_id=1, source_target_pairs={{0,3},{1,0},{2,1},{3,2},{4,7},{5,4},{6,5},{7,6},{8,11},{9,8},{10,9... | collective-permute-start | bytes 983048 | tf_op jit(solution)/shard_map/ppermute | solution.py:380
  149.0 3.8 %collective-permute-done.30 = bf16[128,1280]{1,0:T(8,128)(2,1)S(1)} collective-permute-done((bf16[128,1280]{1,0:T(8,128)(2,1)S(1)}, bf16[128,1280]{1,0:T(8,128)(2,1)S(1)}, u32[]{:S(2)}, u32[]{:S(2)}) %collective-permute-start.30) | collective-permute-done | bytes 327712 | tf_op jit(solution)/shard_map/ppermute | solution.py:380
  153.0 3.8 %collective-permute-start.31 = (bf16[256,1280]{1,0:T(8,128)(2,1)S(1)}, bf16[256,1280]{1,0:T(8,128)(2,1)S(1)}, u32[]{:S(2)}, u32[]{:S(2)}) collective-permute-start(bf16[256,1280]{1,0:T(8,128)(2,1)S(1)} %pad_maximum_fusion.4), channel_id=1, source_target_pairs={{0,3},{1,0},{2,1},{3,2},{4,7},{5,4},{6,5},{7,6},{8,11},{9,8},{10,9... | collective-permute-start | bytes 1966088 | tf_op jit(solution)/shard_map/ppermute | solution.py:386
  158.3 11.3 %collective-permute-done.31 = bf16[256,1280]{1,0:T(8,128)(2,1)S(1)} collective-permute-done((bf16[256,1280]{1,0:T(8,128)(2,1)S(1)}, bf16[256,1280]{1,0:T(8,128)(2,1)S(1)}, u32[]{:S(2)}, u32[]{:S(2)}) %collective-permute-start.31) | collective-permute-done | bytes 655392 | tf_op jit(solution)/shard_map/ppermute | solution.py:386
  169.6 3.6 %collective-permute-done.29 = bf16[256,1280]{1,0:T(8,128)(2,1)S(1)} collective-permute-done((bf16[256,1280]{1,0:T(8,128)(2,1)S(1)}, bf16[256,1280]{1,0:T(8,128)(2,1)S(1)}, u32[]{:S(2)}, u32[]{:S(2)}) %collective-permute-start.29) | collective-permute-done | bytes 655392 | tf_op jit(solution)/shard_map/ppermute | solution.py:385
  (112 shorter events, 52.6 us)
Async XLA Ops:
  1.1 12.2 %collective-permute-start.2 = (bf16[128,1280]{1,0:T(8,128)(2,1)S(1)}, bf16[128,1280]{1,0:T(8,128)(2,1)S(1)}, u32[]{:S(2)}, u32[]{:S(2)}) collective-permute-start(bf16[128,1280]{1,0:T(8,128)(2,1)S(1)} %get-tuple-element.64), channel_id=1, source_target_pairs={{0,2},{1,3},{2,0},{3,1},{4,6},{5,7},{6,4},{7,5},{8,10},{9,11},{10,... | collective-permute-start | bytes 983048 | tf_op jit(solution)/shard_map/ppermute | solution.py:281
  4.3 15.1 %collective-permute-start.1 = (bf16[128,1280]{1,0:T(8,128)(2,1)S(1)}, bf16[128,1280]{1,0:T(8,128)(2,1)S(1)}, u32[]{:S(2)}, u32[]{:S(2)}) collective-permute-start(bf16[128,1280]{1,0:T(8,128)(2,1)S(1)} %get-tuple-element.64), channel_id=1, source_target_pairs={{0,3},{1,0},{2,1},{3,2},{4,7},{5,4},{6,5},{7,6},{8,11},{9,8},{10,9... | collective-permute-start | bytes 983048 | tf_op jit(solution)/shard_map/ppermute | solution.py:281
  5.5 13.9 %collective-permute-start = (bf16[128,1280]{1,0:T(8,128)(2,1)S(1)}, bf16[128,1280]{1,0:T(8,128)(2,1)}, u32[]{:S(2)}, u32[]{:S(2)}) collective-permute-start(bf16[128,1280]{1,0:T(8,128)(2,1)S(1)} %get-tuple-element.64), channel_id=1, source_target_pairs={{0,1},{1,2},{2,3},{3,0},{4,5},{5,6},{6,7},{7,4},{8,9},{9,10},{10,1... | collective-permute-start | bytes 983048 | tf_op jit(solution)/shard_map/ppermute | solution.py:281
  6.3 18.3 %collective-permute-start.5 = (bf16[128,1280]{1,0:T(8,128)(2,1)S(1)}, bf16[128,1280]{1,0:T(8,128)(2,1)S(1)}, u32[]{:S(2)}, u32[]{:S(2)}) collective-permute-start(bf16[128,1280]{1,0:T(8,128)(2,1)S(1)} %get-tuple-element.63), channel_id=1, source_target_pairs={{0,64},{32,96},{64,0},{96,32},{1,65},{33,97},{65,1},{97,33},{2,66}... | collective-permute-start | bytes 983048 | tf_op jit(solution)/shard_map/ppermute | solution.py:281
  10.2 16.1 %collective-permute-start.4 = (bf16[128,1280]{1,0:T(8,128)(2,1)S(1)}, bf16[128,1280]{1,0:T(8,128)(2,1)S(1)}, u32[]{:S(2)}, u32[]{:S(2)}) collective-permute-start(bf16[128,1280]{1,0:T(8,128)(2,1)S(1)} %get-tuple-element.63), channel_id=1, source_target_pairs={{0,96},{32,0},{64,32},{96,64},{1,97},{33,1},{65,33},{97,65},{2,98}... | collective-permute-start | bytes 983048 | tf_op jit(solution)/shard_map/ppermute | solution.py:281
  13.4 13.7 %collective-permute-start.3 = (bf16[128,1280]{1,0:T(8,128)(2,1)S(1)}, bf16[128,1280]{1,0:T(8,128)(2,1)S(1)}, u32[]{:S(2)}, u32[]{:S(2)}) collective-permute-start(bf16[128,1280]{1,0:T(8,128)(2,1)S(1)} %get-tuple-element.63), channel_id=1, source_target_pairs={{0,32},{32,64},{64,96},{96,0},{1,33},{33,65},{65,97},{97,1},{2,34}... | collective-permute-start | bytes 983048 | tf_op jit(solution)/shard_map/ppermute | solution.py:281
  20.6 32.5 %collective-permute-start.7 = (bf16[128,5120]{1,0:T(8,128)(2,1)S(1)}, bf16[128,5120]{1,0:T(8,128)(2,1)}, u32[]{:S(2)}, u32[]{:S(2)}) collective-permute-start(bf16[128,5120]{1,0:T(8,128)(2,1)S(1)} %pad_maximum_fusion.refs_0_), channel_id=1, source_target_pairs={{0,96},{32,0},{64,32},{96,64},{1,97},{33,1},{65,33},{97,65},{2,98}... | collective-permute-start | bytes 3932168 | tf_op jit(solution)/shard_map/ppermute | solution.py:324
  24.7 44.3 %collective-permute-start.6 = (bf16[128,5120]{1,0:T(8,128)(2,1)S(1)}, bf16[128,5120]{1,0:T(8,128)(2,1)}, u32[]{:S(2)}, u32[]{:S(2)}) collective-permute-start(bf16[128,5120]{1,0:T(8,128)(2,1)S(1)} %pad_maximum_fusion.refs_0_), channel_id=1, source_target_pairs={{0,32},{32,64},{64,96},{96,0},{1,33},{33,65},{65,97},{97,1},{2,34}... | collective-permute-start | bytes 3932168 | tf_op jit(solution)/shard_map/ppermute | solution.py:322
  28.1 35.8 %collective-permute-start.12 = (bf16[512,1280]{1,0:T(8,128)(2,1)S(1)}, bf16[512,1280]{1,0:T(8,128)(2,1)}, u32[]{:S(2)}, u32[]{:S(2)}) collective-permute-start(bf16[512,1280]{1,0:T(8,128)(2,1)S(1)} %pad_maximum_fusion.1.refs_1_), channel_id=1, source_target_pairs={{0,3},{1,0},{2,1},{3,2},{4,7},{5,4},{6,5},{7,6},{8,11},{9,8},{10,9... | collective-permute-start | bytes 3932168 | tf_op jit(solution)/shard_map/ppermute | solution.py:325
  30.2 37.5 %collective-permute-start.10 = (bf16[512,1280]{1,0:T(8,128)(2,1)S(1)}, bf16[512,1280]{1,0:T(8,128)(2,1)}, u32[]{:S(2)}, u32[]{:S(2)}) collective-permute-start(bf16[512,1280]{1,0:T(8,128)(2,1)S(1)} %pad_maximum_fusion.1.refs_1_), channel_id=1, source_target_pairs={{0,1},{1,2},{2,3},{3,0},{4,5},{5,6},{6,7},{7,4},{8,9},{9,10},{10,1... | collective-permute-start | bytes 3932168 | tf_op jit(solution)/shard_map/ppermute | solution.py:323
  54.2 24.9 %collective-permute-start.9 = (bf16[64,5120]{1,0:T(8,128)(2,1)S(1)}, bf16[64,5120]{1,0:T(8,128)(2,1)S(1)}, u32[]{:S(2)}, u32[]{:S(2)}) collective-permute-start(bf16[64,5120]{1,0:T(8,128)(2,1)S(1)} %slice.88), channel_id=1, source_target_pairs={{0,96},{32,0},{64,32},{96,64},{1,97},{33,1},{65,33},{97,65},{2,98}... | collective-permute-start | bytes 1966088 | tf_op jit(solution)/shard_map/ppermute | solution.py:330
  65.0 18.0 %collective-permute-start.13 = (bf16[256,1280]{1,0:T(8,128)(2,1)S(1)}, bf16[256,1280]{1,0:T(8,128)(2,1)S(1)}, u32[]{:S(2)}, u32[]{:S(2)}) collective-permute-start(bf16[256,1280]{1,0:T(8,128)(2,1)S(1)} %slice.90), channel_id=1, source_target_pairs={{0,3},{1,0},{2,1},{3,2},{4,7},{5,4},{6,5},{7,6},{8,11},{9,8},{10,9... | collective-permute-start | bytes 1966088 | tf_op jit(solution)/shard_map/ppermute | solution.py:332
  68.9 16.5 %collective-permute-start.11 = (bf16[256,1280]{1,0:T(8,128)(2,1)S(1)}, bf16[256,1280]{1,0:T(8,128)(2,1)S(1)}, u32[]{:S(2)}, u32[]{:S(2)}) collective-permute-start(bf16[256,1280]{1,0:T(8,128)(2,1)S(1)} %slice.89), channel_id=1, source_target_pairs={{0,1},{1,2},{2,3},{3,0},{4,5},{5,6},{6,7},{7,4},{8,9},{9,10},{10,1... | collective-permute-start | bytes 1966088 | tf_op jit(solution)/shard_map/ppermute | solution.py:331
  70.2 16.5 %collective-permute-start.8 = (bf16[64,5120]{1,0:T(8,128)(2,1)S(1)}, bf16[64,5120]{1,0:T(8,128)(2,1)S(1)}, u32[]{:S(2)}, u32[]{:S(2)}) collective-permute-start(bf16[64,5120]{1,0:T(8,128)(2,1)S(1)} %slice.66), channel_id=1, source_target_pairs={{0,32},{32,64},{64,96},{96,0},{1,33},{33,65},{65,97},{97,1},{2,34}... | collective-permute-start | bytes 1966088 | tf_op jit(solution)/shard_map/ppermute | solution.py:329
  76.0 13.6 %collective-permute-start.16 = (bf16[768,256]{1,0:T(8,128)(2,1)S(1)}, bf16[768,256]{1,0:T(8,128)(2,1)S(1)}, u32[]{:S(2)}, u32[]{:S(2)}) collective-permute-start(bf16[768,256]{1,0:T(8,128)(2,1)S(1)} %pad_maximum_fusion.6.refs_0_), channel_id=1, source_target_pairs={{0,24},{4,28},{8,0},{12,4},{16,8},{20,12},{24,16},{28,20},{1,25},{... | collective-permute-start | bytes 1179656 | tf_op jit(solution)/shard_map/ppermute | solution.py:339
  79.1 12.1 %collective-permute-start.15 = (bf16[768,256]{1,0:T(8,128)(2,1)S(1)}, bf16[768,256]{1,0:T(8,128)(2,1)S(1)}, u32[]{:S(2)}, u32[]{:S(2)}) collective-permute-start(bf16[768,256]{1,0:T(8,128)(2,1)S(1)} %pad_maximum_fusion.6.refs_0_), channel_id=1, source_target_pairs={{0,8},{4,12},{8,16},{12,20},{16,24},{20,28},{24,0},{28,4},{1,9},{5... | collective-permute-start | bytes 1179656 | tf_op jit(solution)/shard_map/ppermute | solution.py:339
  93.2 17.6 %collective-permute-start.19 = (bf16[1280,256]{1,0:T(8,128)(2,1)S(1)}, bf16[1280,256]{1,0:T(8,128)(2,1)S(1)}, u32[]{:S(2)}, u32[]{:S(2)}) collective-permute-start(bf16[1280,256]{1,0:T(8,128)(2,1)S(1)} %pad_maximum_fusion.2.refs_3_), channel_id=1, source_target_pairs={{0,24},{4,28},{8,0},{12,4},{16,8},{20,12},{24,16},{28,20},{1,25},{... | collective-permute-start | bytes 1966088 | tf_op jit(solution)/shard_map/ppermute | solution.py:339
  94.8 18.9 %collective-permute-start.18 = (bf16[1280,256]{1,0:T(8,128)(2,1)S(1)}, bf16[1280,256]{1,0:T(8,128)(2,1)S(1)}, u32[]{:S(2)}, u32[]{:S(2)}) collective-permute-start(bf16[1280,256]{1,0:T(8,128)(2,1)S(1)} %pad_maximum_fusion.2.refs_3_), channel_id=1, source_target_pairs={{0,8},{4,12},{8,16},{12,20},{16,24},{20,28},{24,0},{28,4},{1,9},{5... | collective-permute-start | bytes 1966088 | tf_op jit(solution)/shard_map/ppermute | solution.py:339
  104.3 10.8 %collective-permute-start.21 = (bf16[384,256]{1,0:T(8,128)(2,1)S(1)}, bf16[384,256]{1,0:T(8,128)(2,1)S(1)}, u32[]{:S(2)}, u32[]{:S(2)}) collective-permute-start(bf16[384,256]{1,0:T(8,128)(2,1)S(1)} %slice.75), channel_id=1, source_target_pairs={{0,24},{4,28},{8,0},{12,4},{16,8},{20,12},{24,16},{28,20},{1,25},{... | collective-permute-start | bytes 589832 | tf_op jit(solution)/shard_map/ppermute | solution.py:343
  110.8 15.2 %collective-permute-start.23 = (bf16[640,256]{1,0:T(8,128)(2,1)S(1)}, bf16[640,256]{1,0:T(8,128)(2,1)S(1)}, u32[]{:S(2)}, u32[]{:S(2)}) collective-permute-start(bf16[640,256]{1,0:T(8,128)(2,1)S(1)} %slice.96), channel_id=1, source_target_pairs={{0,24},{4,28},{8,0},{12,4},{16,8},{20,12},{24,16},{28,20},{1,25},{... | collective-permute-start | bytes 983048 | tf_op jit(solution)/shard_map/ppermute | solution.py:343
  113.7 12.4 %collective-permute-start.22 = (bf16[640,256]{1,0:T(8,128)(2,1)S(1)}, bf16[640,256]{1,0:T(8,128)(2,1)S(1)}, u32[]{:S(2)}, u32[]{:S(2)}) collective-permute-start(bf16[640,256]{1,0:T(8,128)(2,1)S(1)} %slice.95), channel_id=1, source_target_pairs={{0,8},{4,12},{8,16},{12,20},{16,24},{20,28},{24,0},{28,4},{1,9},{5... | collective-permute-start | bytes 983048 | tf_op jit(solution)/shard_map/ppermute | solution.py:343
  146.1 10.6 %collective-permute-start.28 = (bf16[128,1280]{1,0:T(8,128)(2,1)S(1)}, bf16[128,1280]{1,0:T(8,128)(2,1)S(1)}, u32[]{:S(2)}, u32[]{:S(2)}) collective-permute-start(bf16[128,1280]{1,0:T(8,128)(2,1)S(1)} %get-tuple-element.61), channel_id=1, source_target_pairs={{0,1},{1,2},{2,3},{3,0},{4,5},{5,6},{6,7},{7,4},{8,9},{9,10},{10,1... | collective-permute-start | bytes 983048 | tf_op jit(solution)/shard_map/ppermute | solution.py:379
  153.0 16.6 %collective-permute-start.31 = (bf16[256,1280]{1,0:T(8,128)(2,1)S(1)}, bf16[256,1280]{1,0:T(8,128)(2,1)S(1)}, u32[]{:S(2)}, u32[]{:S(2)}) collective-permute-start(bf16[256,1280]{1,0:T(8,128)(2,1)S(1)} %pad_maximum_fusion.4), channel_id=1, source_target_pairs={{0,3},{1,0},{2,1},{3,2},{4,7},{5,4},{6,5},{7,6},{8,11},{9,8},{10,9... | collective-permute-start | bytes 1966088 | tf_op jit(solution)/shard_map/ppermute | solution.py:386
  156.9 16.3 %collective-permute-start.29 = (bf16[256,1280]{1,0:T(8,128)(2,1)S(1)}, bf16[256,1280]{1,0:T(8,128)(2,1)S(1)}, u32[]{:S(2)}, u32[]{:S(2)}) collective-permute-start(bf16[256,1280]{1,0:T(8,128)(2,1)S(1)} %pad_maximum_fusion.3), channel_id=1, source_target_pairs={{0,1},{1,2},{2,3},{3,0},{4,5},{5,6},{6,7},{7,4},{8,9},{9,10},{10,1... | collective-permute-start | bytes 1966088 | tf_op jit(solution)/shard_map/ppermute | solution.py:385
  (17 other events, 136.3 us)
